TPU v7x, 512 devices: a whole 4x4x16 slice. The times are simulated.
512 devices in a mesh: atom: 64 (over z_hi, x, y, core), kvec: 8 (over z_lo).
Axes of the slice: x: 4, y: 4, z: 16 (z_hi: 2, z_lo: 8; z = z_hi * 8 + z_lo), core: 2. Of those that a mesh axis runs over, the one named last changes fastest.
Arguments:
- atom_coordinates: float32 [3, 131072], P(None, 'atom'), may hold values from 0 to 140
- hidden_atom_loads: float32 [8, 131072], P(None, 'atom'), may hold values from -6 to 6
- lattice_dual_points: float32 [3, 8192], P(None, 'kvec'), may hold values from -2 to 2
- screened_dual_factors: float32 [8192], P('kvec'), as said below
- loss_slope_per_lane: float32 [8], replicated, may hold values from 0.25 to 1.75
Outputs:
- charge_grad: float32 [8, 131072], P(None, ('atom', 'kvec'))
- forces: float32 [3, 131072], P(None, ('atom', 'kvec'))
- energy: float32 [8], replicated
Inputs may be any that keep to these rules, and one draw needn't show every extreme that they name: `screened_dual_factors`: positive.
All inputs are finite; a program needn't handle non-finite values.
Results may differ from a plain program's by a relative error of at most 0.0003.
Values sent between devices are 32-bit elements; how exact they have to be, the bound alone decides.
No kernel may reach another device: no remote copies, remote signals or barrier semaphores. Data moves between devices by JAX's collectives and lax.ppermute only.
A program may use at most 64 MiB of HBM per device.

v0:
```python
import jax
import jax.numpy as jnp
from jax import lax
from jax.sharding import PartitionSpec as P

HIGHEST = lax.Precision.HIGHEST


def phase_angles(kspace_tile, pos):
    theta = kspace_tile[0][:, None] * pos[0][None, :] + kspace_tile[1][:, None] * pos[1][None, :]
    theta = theta + kspace_tile[2][:, None] * pos[2][None, :]
    return (jnp.cos(theta), jnp.sin(theta))


def energy_terms(factors, weights):
    return jnp.sum(weights[None, :] * (factors[0] * factors[0] + factors[1] * factors[1]), axis=1)


def shards(
    atom_coordinates,
    hidden_atom_loads,
    lattice_dual_points,
    screened_dual_factors,
    loss_slope_per_lane,
):
    local_atoms = atom_coordinates.shape[1]
    kept_dual_points = lattice_dual_points.shape[1]
    channels = hidden_atom_loads.shape[0]
    dual_point_tile = 256
    tile_number = kept_dual_points // dual_point_tile
    pieces = []
    for tile_position_id in range(tile_number):
        cosine_terms, sine_terms = phase_angles(
            lattice_dual_points[
                :, tile_position_id * dual_point_tile : (tile_position_id + 1) * dual_point_tile
            ],
            atom_coordinates,
        )
        real_part = jnp.einsum("cn,kn->ck", hidden_atom_loads, cosine_terms, precision=HIGHEST)
        imag_part = jnp.einsum("cn,kn->ck", hidden_atom_loads, sine_terms, precision=HIGHEST)
        pieces.append(jnp.stack([real_part, imag_part]))
    partial_factors = jnp.concatenate(pieces, axis=2)
    all_atoms = local_atoms * lax.axis_size("atom")
    factors = lax.psum(partial_factors, "atom")
    energy = lax.psum(energy_terms(factors, screened_dual_factors), "kvec") / all_atoms
    coefs = (
        2.0 * loss_slope_per_lane[None, :, None] * screened_dual_factors[None, None, :] * factors
    )
    grad_q = jnp.zeros((channels, local_atoms), jnp.float32)
    force = jnp.zeros((3, local_atoms), jnp.float32)
    for tile_position_id in range(tile_number):
        kspace_tile = lattice_dual_points[
            :, tile_position_id * dual_point_tile : (tile_position_id + 1) * dual_point_tile
        ]
        coef_real = coefs[
            0, :, tile_position_id * dual_point_tile : (tile_position_id + 1) * dual_point_tile
        ]
        coef_imag = coefs[
            1, :, tile_position_id * dual_point_tile : (tile_position_id + 1) * dual_point_tile
        ]
        cosine_terms, sine_terms = phase_angles(kspace_tile, atom_coordinates)
        grad_q = (
            grad_q
            + jnp.einsum("ck,kn->cn", coef_real, cosine_terms, precision=HIGHEST)
            + jnp.einsum("ck,kn->cn", coef_imag, sine_terms, precision=HIGHEST)
        )
        along_real = jnp.einsum("ck,cn->kn", coef_real, hidden_atom_loads, precision=HIGHEST)
        along_imag = jnp.einsum("ck,cn->kn", coef_imag, hidden_atom_loads, precision=HIGHEST)
        dtheta = along_imag * cosine_terms - along_real * sine_terms
        force = force - jnp.einsum("dk,kn->dn", kspace_tile, dtheta, precision=HIGHEST)
    partial_grads = jnp.concatenate([grad_q, force], axis=0)
    summed = lax.psum(partial_grads, "kvec")
    owned = local_atoms // lax.axis_size("kvec")
    result = lax.dynamic_slice_in_dim(summed, lax.axis_index("kvec") * owned, owned, 1)
    return (result[:channels], result[channels:], energy)


def solution(mesh):
    return jax.shard_map(
        shards,
        mesh=mesh,
        in_specs=(P(None, "atom"), P(None, "atom"), P(None, "kvec"), P("kvec"), P()),
        out_specs=(P(None, ("atom", "kvec")), P(None, ("atom", "kvec")), P()),
        check_vma=False,
    )
```

profile of v0, /device:TPU:1, one launch (start us, length us, event | category | flops | bytes accessed | tf_op | source)
XLA Modules:
  0.0 1355.3 jit_solution(2528037192682567442)
XLA Ops:
  9.0 8.7 fusion.56
  17.7 9.1 fusion.59
  26.8 8.9 fusion.50
  35.7 8.6 fusion.53
  44.3 8.9 fusion.44
  53.2 9.0 fusion.47
  62.3 8.9 fusion.38
  71.2 8.6 fusion.41
  80.7 1005.3 %all-reduce.3.cloned.1.call-done = f32[2,8,1024]{2,1,0:T(8,128)} async-done(((f32[2,8,1024]{2,1,0:T(8,128)}), f32[2,8,1024]{2,1,0:T(8,128)}) %all-reduce.3.cloned.1.call-update) | async-done | bytes 65552 | tf_op jit(solution)/shard_map/psum | solution.py:44
  1087.9 8.7 convolution_multiply_fusion.7
  1096.5 9.1 convolution_multiply_fusion.5
  1105.6 8.8 convolution_multiply_fusion.3
  1114.5 8.7 convolution_multiply_fusion.1
  1123.1 8.3 fusion.31
  1131.4 9.2 fusion.3
  1141.8 9.0 fusion.2
  1150.8 8.8 fusion.1
  1159.6 9.0 fusion
  1168.6 8.6 convolution_add_fusion.6
  1185.3 8.3 convolution_add_fusion.4
  1210.1 8.5 convolution_add_fusion.1
  1218.6 8.3 convolution_add_fusion
  1231.3 22.5 %psum.23 = f32[8]{0:T(128)S(1)} all-reduce(f32[8]{0:T(128)S(1)} %get-tuple-element.18), channel_id=1, replica_groups=mesh['atom'=64,'kvec'=8] {'kvec'}, use_global_device_ids=true, to_apply=%region_3.0 | all-reduce | flops 8 | bytes 64 | tf_op jit(solution)/shard_map/psum | solution.py:45
  1254.3 91.4 %all-reduce.5.cloned.1.call-done = f32[11,2048]{1,0:T(8,128)} async-done(((f32[11,2048]{1,0:T(8,128)}), f32[11,2048]{1,0:T(8,128)}) %all-reduce.5.cloned.1.call-update) | async-done | bytes 90128 | tf_op jit(solution)/shard_map/psum | solution.py:72
  (29 shorter events, 37.7 us)
Async XLA Ops:
  7.2 1.8 copy-start
  7.2 1078.9 %all-reduce.3.cloned.1.call-start = ((), (), s32[]{:S(2)}) async-start(), calls=%async_computation | async-start | bytes 131072 | tf_op jit(solution)/shard_map/psum | solution.py:44
  71.1 9.6 copy-start.3
  71.1 1014.9 %copy-start.2 = (f32[1024]{0:T(1024)S(1)}, f32[1024]{0:T(1024)}, u32[]{:S(2)}) copy-start(f32[1024]{0:T(1024)} %param.8) | copy-start | bytes 12292
  80.5 1265.2 %all-reduce.5.cloned.1.call-start = ((), (), s32[]{:S(2)}) async-start(), calls=%async_computation.1 | async-start | bytes 262144 | tf_op jit(solution)/shard_map/psum | solution.py:72
  1131.4 9.2 copy-start.1
Sparse Core Ops, SparseCore 0:
  80.6 1005.4 all-reduce.2
  1231.4 114.2 all-reduce.4
where the time goes:
time: 1370 us; the launch traced here: 1360 us
  waiting for transfers between devices  1100 us (80%)
  matrix products  213 us (16%)
  blocking collectives  22.5 us (2%)
  between operations  14.3 us (1%)
    psum x1, waiting for transfers between devices, shards(): factors = lax.psum(partial_factors, 'atom')  1010 us
    psum x1, waiting for transfers between devices, shards(): summed = lax.psum(partial_grads, 'kvec')  91.4 us
    dot_general x4, matrix products, shards(): jnp.einsum('ck,cn->kn', coef_real, hidden_atom_loads, precision=HIGHEST)  36 us
    dot_general x4, matrix products, shards(): jnp.einsum('cn,kn->ck', hidden_atom_loads, cosine_terms, precision=HIGHEST)  35.4 us
    dot_general x4, matrix products, shards(): jnp.einsum('cn,kn->ck', hidden_atom_loads, sine_terms, precision=HIGHEST)  35.4 us
    dot_general x4, matrix products, shards(): jnp.einsum('ck,cn->kn', coef_imag, hidden_atom_loads, precision=HIGHEST)  35.2 us
    dot_general x4, matrix products, shards(): jnp.einsum('ck,kn->cn', coef_imag, sine_terms, precision=HIGHEST)  33.5 us
    dot_general x4, matrix products, shards(): jnp.einsum('ck,kn->cn', coef_real, cosine_terms, precision=HIGHEST)  33.2 us
  transfers between devices with their start and end apart: 2, of which 2 were waited for; matrix products, arithmetic and copies ran while one was open for 0% of the time, Pallas kernels for 0%

commit v1 on v0

v1 whole, which is shorter than its diff:
```python
import functools

import jax
import jax.numpy as jnp
import numpy as np
from jax import lax
from jax.experimental import pallas as pl
from jax.experimental.pallas import tpu as pltpu
from jax.sharding import Mesh
from jax.sharding import PartitionSpec as P

BF16 = jnp.bfloat16
F32 = jnp.float32
PLANE = ("x", "y", "c")
COLUMN = ("zh", "k")
CENTRE = 70.0
SINE = (4.442867755889893, -7.307443618774414, 3.594788074493408, -0.7843739986419678)
COSINE = (1.4142041206359863, -6.977642059326172, 5.715238571166992, -1.7283486127853394)


def halves(value):
    high = value.astype(BF16)
    return high, (value - high.astype(F32)).astype(BF16)


def pieces(value):
    first = value.astype(BF16)
    rest = value - first.astype(F32)
    second = rest.astype(BF16)
    return first, second, (rest - second.astype(F32)).astype(BF16)


def spread(value, outer):
    a, b, c = pieces(value)
    rows = [a, a, a, b, b, b, c, c, c] if outer else [a, b, c] * 3
    return jnp.concatenate(rows + [jnp.zeros((5, value.shape[1]), BF16)], axis=0)


def rows_by_rows(a, b):
    return lax.dot_general(a, b, (((0,), (0,)), ((), ())), preferred_element_type=F32)


def product(a, b):
    return lax.dot_general(a, b, (((1,), (0,)), ((), ())), preferred_element_type=F32)


def polynomial(z, terms):
    total = terms[-1]
    for term in terms[-2::-1]:
        total = term + z * total
    return total


def versine_and_sine(turns):
    g = turns - jnp.round(turns)
    z = g * g
    s = g * polynomial(z, SINE)
    c = polynomial(z, COSINE)
    return s * s, s * c


def structure_kernel(pos_ref, load_ref, dual_ref, out_ref, p_ref, q_ref, w_ref, *, bm, bn):
    atoms, vectors = pos_ref.shape[1], dual_ref.shape[1]
    p_ref[...] = spread(pos_ref[...] - CENTRE, True)
    q_ref[...] = spread(dual_ref[...] * (0.5 / np.pi), False)
    load = load_ref[...]
    w_ref[...] = jnp.concatenate(halves(load), axis=0)
    total = jnp.sum(load, axis=1, keepdims=True)
    for j in range(vectors // bn):
        q = q_ref[:, j * bn : (j + 1) * bn]
        by_versine = jnp.zeros((16, bn), F32)
        by_sine = jnp.zeros((16, bn), F32)
        for i in range(atoms // bm):
            versine, sine = versine_and_sine(rows_by_rows(p_ref[:, i * bm : (i + 1) * bm], q))
            w = w_ref[:, i * bm : (i + 1) * bm]
            for part in halves(versine):
                by_versine = by_versine + product(w, part)
            for part in halves(sine):
                by_sine = by_sine + product(w, part)
        real = total - (by_versine[:8] + by_versine[8:])
        imag = by_sine[:8] + by_sine[8:]
        factors = jnp.concatenate([real, imag], axis=0)
        for t in range(bn // 128):
            out_ref[pl.ds((j * bn + t * 128) // 8, 16), :] = factors[:, t * 128 : (t + 1) * 128]


def structure(pos, load, dual):
    atoms, vectors = pos.shape[1], dual.shape[1]
    return pl.pallas_call(
        functools.partial(structure_kernel, bm=512, bn=256),
        out_shape=jax.ShapeDtypeStruct((vectors // 8, 128), F32),
        in_specs=[pl.BlockSpec(memory_space=pltpu.VMEM)] * 3,
        out_specs=pl.BlockSpec(memory_space=pltpu.VMEM),
        scratch_shapes=[
            pltpu.VMEM((32, atoms), BF16),
            pltpu.VMEM((32, vectors), BF16),
            pltpu.VMEM((16, atoms), BF16),
        ],
        compiler_params=pltpu.CompilerParams(vmem_limit_bytes=40 * 2**20),
        name="structure",
    )(pos, load, dual)


def gradient_kernel(
    table_ref, pos_ref, load_ref, slope_ref, grad_ref, force_ref, energy_ref, p_ref, versine_ref, sine_ref, *, all_atoms, bm
):
    owned = pos_ref.shape[1]
    vectors = p_ref.shape[1]
    q = spread(pos_ref[...] - CENTRE, False)
    load = load_ref[...]
    slope = 2.0 * slope_ref[...]
    energy = jnp.zeros((8, 128), F32)
    constant = jnp.zeros((32, 128), F32)
    for g in range(vectors // 1024):
        for zl in range(8):
            rows = [
                table_ref[pl.ds((g * 4 + part) * 40 + zl, 4, stride=8), :] for part in range(4)
            ]
            dual = table_ref[pl.ds(g * 160 + 32 + zl, 4, stride=40), :]
            real = jnp.concatenate(rows[:2], axis=0)
            imag = jnp.concatenate(rows[2:], axis=0)
            weight = dual[3:4]
            energy = energy + weight * (real * real + imag * imag)
            real = slope * (weight * real)
            imag = slope * (weight * imag)
            at_cosine = jnp.concatenate([-real] + [dual[d : d + 1] * imag for d in range(3)], axis=0)
            at_sine = jnp.concatenate([imag] + [dual[d : d + 1] * real for d in range(3)], axis=0)
            constant = constant - at_cosine
            at = pl.ds((g * 8 + zl) * 128, 128)
            versine_ref[:, at] = jnp.concatenate(halves(at_cosine), axis=0)
            sine_ref[:, at] = jnp.concatenate(halves(at_sine), axis=0)
            p_ref[:, at] = spread(dual[:3] * (0.5 / np.pi), True)
    energy_ref[...] = jnp.sum(energy, axis=1, keepdims=True) * (1.0 / all_atoms)
    total = jnp.zeros((64, owned), F32)
    rest = jnp.zeros((32, owned), F32)
    for i in range(vectors // bm):
        at = slice(i * bm, (i + 1) * bm)
        versine, sine = versine_and_sine(rows_by_rows(p_ref[:, at], q))
        for value, ref in ((versine, versine_ref), (sine, sine_ref)):
            high, low = halves(value)
            total = total + product(ref[:, at], high)
            rest = rest + product(ref[:32, at], low)
    out = total[:32] + total[32:] + rest + jnp.sum(constant, axis=1, keepdims=True)
    grad_ref[...] = out[:8]
    force_ref[...] = jnp.concatenate(
        [jnp.sum(load * out[8 * d + 8 : 8 * d + 16], axis=0, keepdims=True) for d in range(3)], axis=0
    )


def gradients(table, pos, load, slope, vectors, all_atoms):
    owned = pos.shape[1]
    return pl.pallas_call(
        functools.partial(gradient_kernel, all_atoms=all_atoms, bm=512),
        out_shape=(
            jax.ShapeDtypeStruct((8, owned), F32),
            jax.ShapeDtypeStruct((3, owned), F32),
            jax.ShapeDtypeStruct((8, 1), F32),
        ),
        in_specs=[pl.BlockSpec(memory_space=pltpu.VMEM)] * 4,
        out_specs=(pl.BlockSpec(memory_space=pltpu.VMEM),) * 3,
        scratch_shapes=[
            pltpu.VMEM((32, vectors), BF16),
            pltpu.VMEM((64, vectors), BF16),
            pltpu.VMEM((64, vectors), BF16),
        ],
        compiler_params=pltpu.CompilerParams(vmem_limit_bytes=40 * 2**20),
        name="gradients",
    )(table, pos, load, slope)


def shards(pos, load, dual, weights, slope):
    owned = pos.shape[1] // lax.axis_size("k")
    mine = lax.axis_index("k") * owned
    own_pos = lax.dynamic_slice_in_dim(pos, mine, owned, 1)
    own_load = lax.dynamic_slice_in_dim(load, mine, owned, 1)
    place = lax.axis_index(PLANE)
    vectors_here = jnp.concatenate([dual, weights[None]], axis=0)
    own_vectors = lax.dynamic_slice(vectors_here, (place % 4, (place // 4) * 128), (1, 128))

    partial = structure(pos, load, dual)
    parts = lax.all_to_all(partial.reshape(32, 4, 128), PLANE, 0, 0, tiled=True)
    block = jnp.concatenate([jnp.sum(parts, axis=0), own_vectors], axis=0)
    column = lax.all_to_all(jnp.broadcast_to(block.reshape(640), (16, 640)), COLUMN, 0, 0, tiled=True)
    column = column.reshape(2, 8, 5, 128)
    block = jnp.concatenate([column[0, :, :4] + column[1, :, :4], column[0, :, 4:]], axis=1)
    block = jnp.transpose(block, (1, 0, 2)).reshape(5120)
    table = lax.all_to_all(jnp.broadcast_to(block, (32, 5120)), PLANE, 0, 0, tiled=True)
    vectors = dual.shape[1] * lax.axis_size("k")
    all_atoms = pos.shape[1] * lax.axis_size(("zh",) + PLANE)
    grad, force, energy = gradients(
        table.reshape(1280, 128), own_pos, own_load, slope.reshape(8, 1), vectors, all_atoms
    )
    return grad, force, energy.reshape(8)


def solution(mesh):
    fine = Mesh(np.asarray(mesh.devices).reshape(2, 4, 4, 2, 8), ("zh",) + PLANE + ("k",))
    atom = ("zh",) + PLANE
    return jax.shard_map(
        shards,
        mesh=fine,
        in_specs=(P(None, atom), P(None, atom), P(None, "k"), P("k"), P()),
        out_specs=(P(None, atom + ("k",)), P(None, atom + ("k",)), P()),
        check_vma=False,
    )
```

time: 1370 us -> 85.2 us (0.06); the launches traced: 1360 us -> 84.6 us
  waiting for transfers between devices: 1100 us -> 17.6 us
  matrix products: 213 us -> 0 us
  Pallas kernels: 0 us -> 19.1 us
  starting transfers between devices: 0.29 us -> 15.7 us
    psum x2 -> x0, waiting for transfers between devices: 1100 us -> none  [the longest x1 1010 us: shards(): factors = lax.psum(partial_factors, 'atom')]
    dot_general x28 -> x0, matrix products: 213 us -> none  [the longest x4 36 us: shards(): jnp.einsum('ck,cn->kn', coef_real, hidden_atom_loads, precision=HIGHEST)]
    all_to_all x0 -> x1, blocking collectives: none -> 24.3 us  [shards(): lax.all_to_all(jnp.broadcast_to(block.reshape(640), (16, 640)), COLUMN, 0...]
    psum x1 -> x0, blocking collectives: 22.5 us -> none  [shards(): lax.psum(energy_terms(factors, screened_dual_factors), 'kvec') / all_atoms]
    pallas_call x0 -> x2, Pallas kernels: none -> 19.1 us  [the longest x1 9.78 us: structure(): pl.pallas_call(functools.partial(structure_kernel, bm=512, bn=256), out_s...]
    all_to_all x0 -> x2, waiting for transfers between devices: none -> 17.6 us  [the longest x1 10.9 us: shards(): lax.all_to_all(jnp.broadcast_to(block, (32, 5120)), PLANE, 0, 0, tiled=True)]
    all_to_all x0 -> x2, starting transfers between devices: none -> 15.7 us  [the longest x1 10.4 us: shards(): parts = lax.all_to_all(partial.reshape(32, 4, 128), PLANE, 0, 0, tiled=True)]
  transfers between devices with their start and end apart: 2 -> 2, of which waited for: 2 -> 2; matrix products, arithmetic and copies ran while one was open for 0% -> 2% of each run, Pallas kernels for 0% -> 0%
where the time goes in v1:
time: 85.2 us; the launch traced here: 84.6 us
  blocking collectives  24.3 us (29%)
  Pallas kernels  19.1 us (22%)
  waiting for transfers between devices  17.6 us (21%)
  starting transfers between devices  15.7 us (18%)
  local copies, waits for them, and re-layouts  6.32 us (7%)
    all_to_all x1, blocking collectives, shards(): lax.all_to_all(jnp.broadcast_to(block.reshape(640), (16, 640)), COLUMN, 0...  24.3 us
    all_to_all x1, waiting for transfers between devices, shards(): lax.all_to_all(jnp.broadcast_to(block, (32, 5120)), PLANE, 0, 0, tiled=True)  10.9 us
    all_to_all x1, starting transfers between devices, shards(): parts = lax.all_to_all(partial.reshape(32, 4, 128), PLANE, 0, 0, tiled=True)  10.4 us
    pallas_call x1, Pallas kernels, structure(): pl.pallas_call(functools.partial(structure_kernel, bm=512, bn=256), out_s...  9.78 us
    pallas_call x1, Pallas kernels, gradients(): pl.pallas_call(functools.partial(gradient_kernel, all_atoms=all_atoms, bm...  9.34 us
    all_to_all x1, waiting for transfers between devices, shards(): parts = lax.all_to_all(partial.reshape(32, 4, 128), PLANE, 0, 0, tiled=True)  6.66 us
    all_to_all x1, starting transfers between devices, shards(): lax.all_to_all(jnp.broadcast_to(block, (32, 5120)), PLANE, 0, 0, tiled=True)  5.32 us
    unnamed x12, local copies, waits for them, and re-layouts  3.65 us
  transfers between devices with their start and end apart: 2, of which 2 were waited for; matrix products, arithmetic and copies ran while one was open for 2% of the time, Pallas kernels for 0%

profile of v1, /device:TPU:1, one launch (start us, length us, event | category | flops | bytes accessed | tf_op | source)
XLA Modules:
  0.0 84.6 jit_solution(15427951088028708741)
XLA Ops:
  0.6 0.0 copy-start
  0.6 0.8 copy-done
  1.5 0.0 copy-start.1
  1.5 0.7 copy-done.1
  2.2 0.8 copy-done.3
  2.9 9.8 %structure.1 = f32[128,128]{1,0:T(8,128)} custom-call(f32[3,2048]{1,0:T(4,128)S(1)} %copy-done.3, f32[8,2048]{1,0:T(8,128)S(1)} %copy-done, f32[3,1024]{1,0:T(4,128)S(1)} %copy-done.1), custom_call_target="tpu_custom_call" | custom-call | tf_op jit(solution)/shard_map/structure/pallas_call | solution.py:89
  12.7 10.4 %all-to-all-start = ((f32[32,4,128]{2,1,0:T(4,128)}), f32[32,4,128]{2,1,0:T(4,128)S(1)}, u32[]{:S(2)}, u32[]{:S(2)}) async-start(f32[32,4,128]{2,1,0:T(4,128)} %bitcast), calls=%async_computation | async-start | bytes 131072 | tf_op jit(solution)/shard_map/all_to_all | solution.py:181
  23.1 0.0 copy-start.2
  23.2 0.0 copy-start.4
  23.2 0.7 copy-done.2
  23.9 0.0 copy-done.4
  23.9 0.1 fusion.1
  23.9 6.7 %all-to-all-done = f32[32,4,128]{2,1,0:T(4,128)S(1)} async-done(((f32[32,4,128]{2,1,0:T(4,128)}), f32[32,4,128]{2,1,0:T(4,128)S(1)}, u32[]{:S(2)}, u32[]{:S(2)}) %all-to-all-start) | async-done | bytes 65568 | tf_op jit(solution)/shard_map/all_to_all | solution.py:181
  30.7 24.3 %all_to_all.17 = f32[16,1,640]{2,1,0:T(1,128)S(1)} all-to-all(f32[16,1,640]{2,1,0:T(1,128)S(1)} %broadcast_in_dim.15), channel_id=1, replica_groups=mesh['zh'=2,'x'=4,'y'=4,'c'=2,'k'=8] {'zh','k'}, dimensions={0} | all-to-all | bytes 81920 | tf_op jit(solution)/shard_map/all_to_all | solution.py:183
  55.1 1.2 %broadcast_in_dim.17 = f32[32,1,5120]{2,1,0:T(1,128)} broadcast(f32[5120]{0:T(1024)S(1)} %maximum_bitcast_fusion), dimensions={2} | broadcast | bytes 675840 | tf_op jit(solution)/shard_map/broadcast_in_dim | solution.py:187
  56.2 5.3 %all-to-all-start.2 = ((f32[32,1,5120]{2,1,0:T(1,128)}), f32[32,1,5120]{2,1,0:T(1,128)S(1)}, u32[]{:S(2)}, u32[]{:S(2)}) async-start(f32[32,1,5120]{2,1,0:T(1,128)} %broadcast_in_dim.17), calls=%async_computation.2 | async-start | bytes 1310720 | tf_op jit(solution)/shard_map/all_to_all | solution.py:187
  61.6 0.0 copy-start.5
  61.6 0.6 copy-done.5
  62.2 0.1 copy.12.slope_ref
  62.3 0.7 constant_dynamic-slice_fusion.1.pos_ref
  63.0 0.7 constant_dynamic-slice_fusion.load_ref
  63.7 10.9 %all-to-all-done.2 = f32[32,1,5120]{2,1,0:T(1,128)S(1)} async-done(((f32[32,1,5120]{2,1,0:T(1,128)}), f32[32,1,5120]{2,1,0:T(1,128)S(1)}, u32[]{:S(2)}, u32[]{:S(2)}) %all-to-all-start.2) | async-done | bytes 655392 | tf_op jit(solution)/shard_map/all_to_all | solution.py:187
  74.6 9.3 %gradients.1 = (f32[8,256]{1,0:T(8,128)}, f32[3,256]{1,0:T(4,128)}, f32[8,1]{1,0:T(8,128)S(1)}) custom-call(f32[1280,128]{1,0:T(8,128)S(1)} %bitcast.17, f32[3,256]{1,0:T(4,128)S(1)} %constant_dynamic-slice_fusion.1.pos_ref, f32[8,256]{1,0:T(8,128)S(1)} %constant_dynamic-slice_fusion.load_ref, f32[8,1]{1,0:T(8,128)S(1)} %copy.12.slope_ref), custom_call_target="tpu_custom_call" | custom-call | tf_op jit(solution)/shard_map/gradients/pallas_call | solution.py:152
  83.9 0.6 reduce
  (8 shorter events, 0.1 us)
Async XLA Ops:
  0.6 0.8 copy-start
  1.5 0.7 copy-start.1
  2.2 0.8 copy-start.3
  12.7 17.9 %all-to-all-start = ((f32[32,4,128]{2,1,0:T(4,128)}), f32[32,4,128]{2,1,0:T(4,128)S(1)}, u32[]{:S(2)}, u32[]{:S(2)}) async-start(f32[32,4,128]{2,1,0:T(4,128)} %bitcast), calls=%async_computation | async-start | bytes 131072 | tf_op jit(solution)/shard_map/all_to_all | solution.py:181
  23.1 0.7 copy-start.2
  23.2 0.7 copy-start.4
  56.2 18.4 %all-to-all-start.2 = ((f32[32,1,5120]{2,1,0:T(1,128)}), f32[32,1,5120]{2,1,0:T(1,128)S(1)}, u32[]{:S(2)}, u32[]{:S(2)}) async-start(f32[32,1,5120]{2,1,0:T(1,128)} %broadcast_in_dim.17), calls=%async_computation.2 | async-start | bytes 1310720 | tf_op jit(solution)/shard_map/all_to_all | solution.py:187
  61.6 0.7 copy-start.5

commit v2 on v1

v2 whole, which is shorter than its diff:
```python
import functools

import jax
import jax.numpy as jnp
import numpy as np
from jax import lax
from jax.experimental import pallas as pl
from jax.experimental.pallas import tpu as pltpu
from jax.sharding import Mesh
from jax.sharding import PartitionSpec as P

BF16 = jnp.bfloat16
F32 = jnp.float32
PLANE = ("x", "y", "c")
COLUMN = ("zh", "k")
CENTRE = 70.0
SINE = (2.2214303016662598, -0.9131746292114258, 0.10983827710151672)


def halves(value):
    high = value.astype(BF16)
    return high, (value - high.astype(F32)).astype(BF16)


def pieces(value):
    first = value.astype(BF16)
    rest = value - first.astype(F32)
    second = rest.astype(BF16)
    return first, second, (rest - second.astype(F32)).astype(BF16)


def spread(value, outer):
    a, b, c = pieces(value)
    rows = [a, a, a, b, b, b, c, c, c] if outer else [a, b, c] * 3
    return jnp.concatenate(rows + [jnp.zeros((5, value.shape[1]), BF16)], axis=0)


def rows_by_rows(a, b):
    return lax.dot_general(a, b, (((0,), (0,)), ((), ())), preferred_element_type=F32)


def product(a, b):
    return lax.dot_general(a, b, (((1,), (0,)), ((), ())), preferred_element_type=F32)


def polynomial(z, terms):
    total = terms[-1]
    for term in terms[-2::-1]:
        total = term + z * total
    return total


def versine_and_sine(turns):
    g = turns - jnp.round(turns)
    s = g * polynomial(g * g, SINE)
    versine = s * s
    square = 2.0 - versine
    sine = s * (square * lax.rsqrt(square))
    return sine * sine, sine * (1.0 - versine)


def pipelined(tiles, phase, trig_weights, turns_ref, trig_ref, step):
    rows = turns_ref.shape[1]

    def elementwise(t):
        for r in range(0, rows, step):
            versine, sine = versine_and_sine(turns_ref[t % 2, r : r + step, :])
            for part, value in enumerate(halves(versine) + halves(sine)):
                trig_ref[t % 2, part, r : r + step, :] = value

    turns_ref[0] = phase(0)
    for t in range(tiles):
        if t + 1 < tiles:
            turns_ref[(t + 1) % 2] = phase(t + 1)
        if t > 0:
            trig_weights(t - 1)
        elementwise(t)
    trig_weights(tiles - 1)


def structure_kernel(
    pos_hbm, load_hbm, dual_hbm, out_ref, pos_ref, load_ref, dual_ref, p_ref, q_ref, w_ref, turns_ref, trig_ref, sems
):
    copies = [
        pltpu.make_async_copy(source, target, sems.at[n])
        for n, (source, target) in enumerate(
            ((dual_hbm, dual_ref), (pos_hbm, pos_ref), (load_hbm, load_ref))
        )
    ]
    for copy in copies:
        copy.start()
    atoms, vectors = pos_ref.shape[1], dual_ref.shape[1]
    bm, bn = turns_ref.shape[1:]
    copies[0].wait()
    q_ref[...] = spread(dual_ref[...] * (0.5 / np.pi), False)
    copies[1].wait()
    p_ref[...] = spread(pos_ref[...] - CENTRE, True)
    copies[2].wait()
    load = load_ref[...]
    w_ref[...] = jnp.concatenate(halves(load), axis=0)
    total = jnp.sum(load, axis=1, keepdims=True)
    tiles = [(i, j) for j in range(vectors // bn) for i in range(atoms // bm)]
    sums = {}

    def phase(t):
        i, j = tiles[t]
        return rows_by_rows(p_ref[:, i * bm : (i + 1) * bm], q_ref[:, j * bn : (j + 1) * bn])

    def weigh(t):
        i, j = tiles[t]
        w = w_ref[:, i * bm : (i + 1) * bm]
        for part in range(4):
            term = product(w, trig_ref[t % 2, part])
            sums[part // 2] = sums[part // 2] + term if part % 2 or i > 0 else term
        if i == atoms // bm - 1:
            real = total - 2.0 * (sums[0][:8] + sums[0][8:])
            imag = 2.0 * (sums[1][:8] + sums[1][8:])
            factors = jnp.concatenate([real, imag], axis=0)
            for lane in range(0, bn, 128):
                out_ref[pl.ds((j * bn + lane) // 8, 16), :] = factors[:, lane : lane + 128]

    pipelined(len(tiles), phase, weigh, turns_ref, trig_ref, 16)


def structure(pos, load, dual):
    atoms, vectors = pos.shape[1], dual.shape[1]
    bm, bn = 512, 256
    return pl.pallas_call(
        structure_kernel,
        out_shape=jax.ShapeDtypeStruct((vectors // 8, 128), F32),
        in_specs=[pl.BlockSpec(memory_space=pl.ANY)] * 3,
        out_specs=pl.BlockSpec(memory_space=pltpu.VMEM),
        scratch_shapes=[
            pltpu.VMEM(pos.shape, F32),
            pltpu.VMEM(load.shape, F32),
            pltpu.VMEM(dual.shape, F32),
            pltpu.VMEM((32, atoms), BF16),
            pltpu.VMEM((32, vectors), BF16),
            pltpu.VMEM((16, atoms), BF16),
            pltpu.VMEM((2, bm, bn), F32),
            pltpu.VMEM((2, 4, bm, bn), BF16),
            pltpu.SemaphoreType.DMA((3,)),
        ],
        compiler_params=pltpu.CompilerParams(vmem_limit_bytes=60 * 2**20),
        name="structure",
    )(pos, load, dual)


def gradient_kernel(
    table_ref,
    pos_ref,
    load_ref,
    slope_ref,
    grad_ref,
    force_ref,
    energy_ref,
    p_ref,
    versine_ref,
    sine_ref,
    turns_ref,
    trig_ref,
    *,
    all_atoms,
):
    bm, owned = turns_ref.shape[1:]
    vectors = p_ref.shape[1]
    q = spread(pos_ref[...] - CENTRE, False)
    load = load_ref[...]
    slope = 2.0 * slope_ref[...]
    sums = {
        "energy": jnp.zeros((8, 128), F32),
        "constant": jnp.zeros((32, 128), F32),
        "high": jnp.zeros((64, owned), F32),
        "low": jnp.zeros((32, owned), F32),
    }

    def duals(b):
        return table_ref[pl.ds((b // 8) * 160 + 32 + b % 8, 4, stride=40), :]

    def weights(b):
        g, zl = b // 8, b % 8
        rows = [table_ref[pl.ds((g * 4 + part) * 40 + zl, 4, stride=8), :] for part in range(4)]
        dual = duals(b)
        real = jnp.concatenate(rows[:2], axis=0)
        imag = jnp.concatenate(rows[2:], axis=0)
        weight = dual[3:4]
        sums["energy"] = sums["energy"] + weight * (real * real + imag * imag)
        real = slope * (weight * real)
        imag = slope * (weight * imag)
        at_cosine = jnp.concatenate([real] + [-dual[d : d + 1] * imag for d in range(3)], axis=0)
        at_sine = jnp.concatenate([imag] + [dual[d : d + 1] * real for d in range(3)], axis=0)
        sums["constant"] = sums["constant"] + at_cosine
        at = pl.ds(b * 128, 128)
        versine_ref[:, at] = jnp.concatenate(halves(-2.0 * at_cosine), axis=0)
        sine_ref[:, at] = jnp.concatenate(halves(2.0 * at_sine), axis=0)

    def phase(t):
        at = slice(t * bm, (t + 1) * bm)
        for b in range(t * bm // 128, (t + 1) * bm // 128):
            p_ref[:, b * 128 : (b + 1) * 128] = spread(duals(b)[:3] * (0.5 / np.pi), True)
        return rows_by_rows(p_ref[:, at], q)

    def weigh(t):
        at = slice(t * bm, (t + 1) * bm)
        for b in range(t * bm // 128, (t + 1) * bm // 128):
            weights(b)
        for part, ref in enumerate((versine_ref, sine_ref)):
            sums["high"] = sums["high"] + product(ref[:, at], trig_ref[t % 2, 2 * part])
            sums["low"] = sums["low"] + product(ref[:32, at], trig_ref[t % 2, 2 * part + 1])

    pipelined(vectors // bm, phase, weigh, turns_ref, trig_ref, 16)
    energy = jnp.sum(sums["energy"], axis=1, keepdims=True) * (1.0 / all_atoms)
    eye = lax.broadcasted_iota(jnp.int32, (8, 8), 0) == lax.broadcasted_iota(jnp.int32, (8, 8), 1)
    energy_ref[...] = jnp.sum(jnp.where(eye, energy, 0.0), axis=0, keepdims=True)
    out = sums["high"][:32] + sums["high"][32:] + sums["low"]
    out = out + jnp.sum(sums["constant"], axis=1, keepdims=True)
    grad_ref[...] = out[:8]
    force_ref[...] = jnp.concatenate(
        [jnp.sum(load * out[8 * d + 8 : 8 * d + 16], axis=0, keepdims=True) for d in range(3)], axis=0
    )


def gradients(table, pos, load, slope, vectors, all_atoms):
    owned = pos.shape[1]
    bm = 512
    return pl.pallas_call(
        functools.partial(gradient_kernel, all_atoms=all_atoms),
        out_shape=(
            jax.ShapeDtypeStruct((8, owned), F32),
            jax.ShapeDtypeStruct((3, owned), F32),
            jax.ShapeDtypeStruct((1, 8), F32),
        ),
        in_specs=[pl.BlockSpec(memory_space=pltpu.VMEM)] * 4,
        out_specs=(pl.BlockSpec(memory_space=pltpu.VMEM),) * 3,
        scratch_shapes=[
            pltpu.VMEM((32, vectors), BF16),
            pltpu.VMEM((64, vectors), BF16),
            pltpu.VMEM((64, vectors), BF16),
            pltpu.VMEM((2, bm, owned), F32),
            pltpu.VMEM((2, 4, bm, owned), BF16),
        ],
        compiler_params=pltpu.CompilerParams(vmem_limit_bytes=40 * 2**20),
        name="gradients",
    )(table, pos, load, slope)


def shards(pos, load, dual, weights, slope):
    owned = pos.shape[1] // lax.axis_size("k")
    mine = lax.axis_index("k") * owned
    own_pos = lax.dynamic_slice_in_dim(pos, mine, owned, 1)
    own_load = lax.dynamic_slice_in_dim(load, mine, owned, 1)
    place = lax.axis_index(PLANE)
    vectors_here = jnp.concatenate([dual, weights[None]], axis=0)
    own_vectors = lax.dynamic_slice(vectors_here, (place % 4, (place // 4) * 128), (1, 128))

    partial = structure(pos, load, dual)
    parts = lax.all_to_all(partial.reshape(32, 4, 128), PLANE, 0, 0, tiled=True)
    block = jnp.concatenate([jnp.sum(parts, axis=0), own_vectors], axis=0)
    column = lax.all_to_all(jnp.broadcast_to(block.reshape(640), (16, 640)), COLUMN, 0, 0, tiled=True)
    column = column.reshape(2, 8, 5, 128)
    block = jnp.concatenate([column[0, :, :4] + column[1, :, :4], column[0, :, 4:]], axis=1)
    block = jnp.transpose(block, (1, 0, 2)).reshape(40, 128)
    table = lax.all_to_all(jnp.broadcast_to(block, (32, 40, 128)), PLANE, 0, 0, tiled=True)
    vectors = dual.shape[1] * lax.axis_size("k")
    all_atoms = pos.shape[1] * lax.axis_size(("zh",) + PLANE)
    grad, force, energy = gradients(
        table.reshape(1280, 128), own_pos, own_load, slope.reshape(8, 1), vectors, all_atoms
    )
    return grad, force, energy.reshape(8)


def solution(mesh):
    fine = Mesh(np.asarray(mesh.devices).reshape(2, 4, 4, 2, 8), ("zh",) + PLANE + ("k",))
    atom = ("zh",) + PLANE
    return jax.shard_map(
        shards,
        mesh=fine,
        in_specs=(P(None, atom), P(None, atom), P(None, "k"), P("k"), P()),
        out_specs=(P(None, atom + ("k",)), P(None, atom + ("k",)), P()),
        check_vma=False,
    )
```

time: 85.2 us -> 80.1 us (0.940)
  local copies, waits for them, and re-layouts: 6.32 us -> 3.72 us
  Pallas kernels: 19.1 us -> 17.4 us
    unnamed x12 -> x6, local copies, waits for them, and re-layouts: 3.65 us -> 1.34 us
    pallas_call x2, Pallas kernels: 19.1 us -> 17.4 us  [the longest x1 9.15 us: gradients(): pl.pallas_call(functools.partial(gradient_kernel, all_atoms=all_atoms), o...]
where the time goes in v2:
time: 80.1 us; the launch traced here: 79.6 us
  blocking collectives  24.3 us (30%)
  waiting for transfers between devices  17.6 us (22%)
  Pallas kernels  17.4 us (22%)
  starting transfers between devices  15.7 us (20%)
  local copies, waits for them, and re-layouts  3.72 us (5%)
    all_to_all x1, blocking collectives, shards(): lax.all_to_all(jnp.broadcast_to(block.reshape(640), (16, 640)), COLUMN, 0...  24.3 us
    all_to_all x1, waiting for transfers between devices, shards(): lax.all_to_all(jnp.broadcast_to(block, (32, 40, 128)), PLANE, 0, 0, tiled...  10.9 us
    all_to_all x1, starting transfers between devices, shards(): parts = lax.all_to_all(partial.reshape(32, 4, 128), PLANE, 0, 0, tiled=True)  10.4 us
    pallas_call x1, Pallas kernels, gradients(): pl.pallas_call(functools.partial(gradient_kernel, all_atoms=all_atoms), o...  9.15 us
    pallas_call x1, Pallas kernels, structure(): pl.pallas_call(structure_kernel, out_shape=jax.ShapeDtypeStruct((vectors...  8.21 us
    all_to_all x1, waiting for transfers between devices, shards(): parts = lax.all_to_all(partial.reshape(32, 4, 128), PLANE, 0, 0, tiled=True)  6.66 us
    all_to_all x1, starting transfers between devices, shards(): lax.all_to_all(jnp.broadcast_to(block, (32, 40, 128)), PLANE, 0, 0, tiled...  5.32 us
  transfers between devices with their start and end apart: 2, of which 2 were waited for; matrix products, arithmetic and copies ran while one was open for 2% of the time, Pallas kernels for 0%

profile of v2, /device:TPU:1, one launch (start us, length us, event | category | flops | bytes accessed | tf_op | source)
XLA Modules:
  0.0 79.6 jit_solution(11949384208938324466)
XLA Ops:
  0.6 8.2 %structure.1 = f32[128,128]{1,0:T(8,128)} custom-call(f32[3,2048]{1,0:T(4,128)} %pos_hbm.1, f32[8,2048]{1,0:T(8,128)} %load_hbm.1, f32[3,1024]{1,0:T(4,128)} %dual_hbm.1), custom_call_target="tpu_custom_call" | custom-call | tf_op jit(solution)/shard_map/structure/pallas_call | solution.py:128
  8.8 10.4 %all-to-all-start = ((f32[32,4,128]{2,1,0:T(4,128)}), f32[32,4,128]{2,1,0:T(4,128)S(1)}, u32[]{:S(2)}, u32[]{:S(2)}) async-start(f32[32,4,128]{2,1,0:T(4,128)} %bitcast.19), calls=%async_computation | async-start | bytes 131072 | tf_op jit(solution)/shard_map/all_to_all | solution.py:257
  19.3 0.0 copy-start
  19.3 0.0 copy-start.1
  19.3 0.7 copy-done
  20.0 0.0 copy-done.1
  20.0 0.1 fusion.1
  20.1 6.7 %all-to-all-done = f32[32,4,128]{2,1,0:T(4,128)S(1)} async-done(((f32[32,4,128]{2,1,0:T(4,128)}), f32[32,4,128]{2,1,0:T(4,128)S(1)}, u32[]{:S(2)}, u32[]{:S(2)}) %all-to-all-start) | async-done | bytes 65568 | tf_op jit(solution)/shard_map/all_to_all | solution.py:257
  26.8 24.3 %all_to_all.16 = f32[16,1,640]{2,1,0:T(1,128)S(1)} all-to-all(f32[16,1,640]{2,1,0:T(1,128)S(1)} %broadcast_in_dim.13), channel_id=1, replica_groups=mesh['zh'=2,'x'=4,'y'=4,'c'=2,'k'=8] {'zh','k'}, dimensions={0} | all-to-all | bytes 81920 | tf_op jit(solution)/shard_map/all_to_all | solution.py:259
  51.2 0.9 %broadcast_in_dim.14 = f32[32,40,128]{2,1,0:T(8,128)} broadcast(f32[40,128]{1,0:T(8,128)S(1)} %maximum_bitcast_fusion), dimensions={1,2} | broadcast | bytes 675840 | tf_op jit(solution)/shard_map/broadcast_in_dim | solution.py:263
  52.1 5.3 %all-to-all-start.2 = ((f32[32,40,128]{2,1,0:T(8,128)}), f32[32,40,128]{2,1,0:T(8,128)S(1)}, u32[]{:S(2)}, u32[]{:S(2)}) async-start(f32[32,40,128]{2,1,0:T(8,128)} %broadcast_in_dim.14), calls=%async_computation.2 | async-start | bytes 1310720 | tf_op jit(solution)/shard_map/all_to_all | solution.py:263
  57.4 0.0 copy-start.2
  57.4 0.6 copy-done.2
  58.0 0.1 copy.11.slope_ref
  58.1 0.7 constant_dynamic-slice_fusion.1.pos_ref
  58.8 0.7 constant_dynamic-slice_fusion.load_ref
  59.5 10.9 %all-to-all-done.2 = f32[32,40,128]{2,1,0:T(8,128)S(1)} async-done(((f32[32,40,128]{2,1,0:T(8,128)}), f32[32,40,128]{2,1,0:T(8,128)S(1)}, u32[]{:S(2)}, u32[]{:S(2)}) %all-to-all-start.2) | async-done | bytes 655392 | tf_op jit(solution)/shard_map/all_to_all | solution.py:263
  70.4 9.1 %gradients.1 = (f32[8,256]{1,0:T(8,128)}, f32[3,256]{1,0:T(4,128)}, f32[1,8]{1,0:T(1,128)}) custom-call(f32[1280,128]{1,0:T(8,128)S(1)} %bitcast.18, f32[3,256]{1,0:T(4,128)S(1)} %constant_dynamic-slice_fusion.1.pos_ref, f32[8,256]{1,0:T(8,128)S(1)} %constant_dynamic-slice_fusion.load_ref, f32[8,1]{1,0:T(8,128)S(1)} %copy.11.slope_ref), custom_call_target="tpu_custom_call" | custom-call | tf_op jit(solution)/shard_map/gradients/pallas_call | solution.py:226
  (7 shorter events, 0.1 us)
Async XLA Ops:
  8.8 17.9 %all-to-all-start = ((f32[32,4,128]{2,1,0:T(4,128)}), f32[32,4,128]{2,1,0:T(4,128)S(1)}, u32[]{:S(2)}, u32[]{:S(2)}) async-start(f32[32,4,128]{2,1,0:T(4,128)} %bitcast.19), calls=%async_computation | async-start | bytes 131072 | tf_op jit(solution)/shard_map/all_to_all | solution.py:257
  19.3 0.7 copy-start
  19.3 0.7 copy-start.1
  52.1 18.4 %all-to-all-start.2 = ((f32[32,40,128]{2,1,0:T(8,128)}), f32[32,40,128]{2,1,0:T(8,128)S(1)}, u32[]{:S(2)}, u32[]{:S(2)}) async-start(f32[32,40,128]{2,1,0:T(8,128)} %broadcast_in_dim.14), calls=%async_computation.2 | async-start | bytes 1310720 | tf_op jit(solution)/shard_map/all_to_all | solution.py:263
  57.4 0.7 copy-start.2

commit v3 on v2

--- a/solution.py
+++ b/solution.py
@@ -13,6 +13,9 @@
 F32 = jnp.float32
 PLANE = ("x", "y", "c")
 COLUMN = ("zh", "k")
+PLANE_FLIP = 20
+CORE_PLANE_FLIP = 10
+COLUMN_ORDER = (*range(8, 16), *range(8))
 CENTRE = 70.0
 SINE = (2.2214303016662598, -0.9131746292114258, 0.10983827710151672)
 
@@ -117,7 +120,12 @@
             imag = 2.0 * (sums[1][:8] + sums[1][8:])
             factors = jnp.concatenate([real, imag], axis=0)
             for lane in range(0, bn, 128):
-                out_ref[pl.ds((j * bn + lane) // 8, 16), :] = factors[:, lane : lane + 128]
+                group = (j * bn + lane) // 128
+                for part in range(4):
+                    place = ((group % 4) * 8 + part * 2 + group // 4) ^ PLANE_FLIP
+                    out_ref[place * 4 : place * 4 + 4, :] = factors[
+                        part * 4 : part * 4 + 4, lane : lane + 128
+                    ]
 
     pipelined(len(tiles), phase, weigh, turns_ref, trig_ref, 16)
 
@@ -146,14 +154,25 @@
     )(pos, load, dual)
 
 
+def spread_four(value, outer):
+    twice = jnp.concatenate([value, value], axis=0)
+    a = twice.astype(BF16).astype(F32)
+    rest = twice - a
+    b = rest.astype(BF16).astype(F32)
+    c = rest - b
+    first = lax.broadcasted_iota(jnp.int32, twice.shape, 0) < 4
+    if outer:
+        rows = [a, jnp.where(first, a, b), b, c]
+    else:
+        rows = [jnp.where(first, a, b), jnp.where(first, c, a), jnp.where(first, b, c), jnp.where(first, a, b)]
+    return jnp.concatenate(rows, axis=0).astype(BF16)
+
+
 def gradient_kernel(
     table_ref,
-    pos_ref,
-    load_ref,
+    atoms_ref,
     slope_ref,
-    grad_ref,
-    force_ref,
-    energy_ref,
+    out_ref,
     p_ref,
     versine_ref,
     sine_ref,
@@ -164,9 +183,12 @@
 ):
     bm, owned = turns_ref.shape[1:]
     vectors = p_ref.shape[1]
-    q = spread(pos_ref[...] - CENTRE, False)
-    load = load_ref[...]
-    slope = 2.0 * slope_ref[...]
+    atoms = jnp.concatenate([atoms_ref[0], atoms_ref[1]], axis=1)
+    load = atoms[:8]
+    pos = jnp.concatenate([atoms[8:11] - CENTRE, jnp.zeros((1, owned), F32)], axis=0)
+    q = spread_four(pos, False)
+    slope = 4.0 * slope_ref[...]
+    is_dual = lax.broadcasted_iota(jnp.int32, (4, 128), 0) < 3
     sums = {
         "energy": jnp.zeros((8, 128), F32),
         "constant": jnp.zeros((32, 128), F32),
@@ -175,29 +197,34 @@
     }
 
     def duals(b):
-        return table_ref[pl.ds((b // 8) * 160 + 32 + b % 8, 4, stride=40), :]
+        places = [((b // 8) * 4 + part) ^ CORE_PLANE_FLIP for part in range(4)]
+        return jnp.concatenate([table_ref[pl.ds(at * 40 + 32 + b % 8, 1), :] for at in places], axis=0)
 
     def weights(b):
         g, zl = b // 8, b % 8
-        rows = [table_ref[pl.ds((g * 4 + part) * 40 + zl, 4, stride=8), :] for part in range(4)]
+        rows = [
+            table_ref[pl.ds(((g * 4 + part) ^ CORE_PLANE_FLIP) * 40 + zl, 4, stride=8), :]
+            for part in range(4)
+        ]
         dual = duals(b)
         real = jnp.concatenate(rows[:2], axis=0)
         imag = jnp.concatenate(rows[2:], axis=0)
         weight = dual[3:4]
-        sums["energy"] = sums["energy"] + weight * (real * real + imag * imag)
-        real = slope * (weight * real)
-        imag = slope * (weight * imag)
-        at_cosine = jnp.concatenate([real] + [-dual[d : d + 1] * imag for d in range(3)], axis=0)
-        at_sine = jnp.concatenate([imag] + [dual[d : d + 1] * real for d in range(3)], axis=0)
-        sums["constant"] = sums["constant"] + at_cosine
+        real_term, imag_term = weight * real, weight * imag
+        sums["energy"] = sums["energy"] + (real_term * real + imag_term * imag)
+        real_term, imag_term = slope * real_term, slope * imag_term
+        at_versine = jnp.concatenate([-real_term] + [dual[d : d + 1] * imag_term for d in range(3)], axis=0)
+        at_sine = jnp.concatenate([imag_term] + [dual[d : d + 1] * real_term for d in range(3)], axis=0)
+        sums["constant"] = sums["constant"] + at_versine
         at = pl.ds(b * 128, 128)
-        versine_ref[:, at] = jnp.concatenate(halves(-2.0 * at_cosine), axis=0)
-        sine_ref[:, at] = jnp.concatenate(halves(2.0 * at_sine), axis=0)
+        versine_ref[:, at] = jnp.concatenate(halves(at_versine), axis=0)
+        sine_ref[:, at] = jnp.concatenate(halves(at_sine), axis=0)
 
     def phase(t):
         at = slice(t * bm, (t + 1) * bm)
         for b in range(t * bm // 128, (t + 1) * bm // 128):
-            p_ref[:, b * 128 : (b + 1) * 128] = spread(duals(b)[:3] * (0.5 / np.pi), True)
+            dual = jnp.where(is_dual, duals(b) * (0.5 / np.pi), 0.0)
+            p_ref[:, b * 128 : (b + 1) * 128] = spread_four(dual, True)
         return rows_by_rows(p_ref[:, at], q)
 
     def weigh(t):
@@ -210,28 +237,26 @@
 
     pipelined(vectors // bm, phase, weigh, turns_ref, trig_ref, 16)
     energy = jnp.sum(sums["energy"], axis=1, keepdims=True) * (1.0 / all_atoms)
-    eye = lax.broadcasted_iota(jnp.int32, (8, 8), 0) == lax.broadcasted_iota(jnp.int32, (8, 8), 1)
-    energy_ref[...] = jnp.sum(jnp.where(eye, energy, 0.0), axis=0, keepdims=True)
+    shape = (8, owned)
+    diagonal = lax.broadcasted_iota(jnp.int32, shape, 0) == lax.broadcasted_iota(jnp.int32, shape, 1)
     out = sums["high"][:32] + sums["high"][32:] + sums["low"]
-    out = out + jnp.sum(sums["constant"], axis=1, keepdims=True)
-    grad_ref[...] = out[:8]
-    force_ref[...] = jnp.concatenate(
-        [jnp.sum(load * out[8 * d + 8 : 8 * d + 16], axis=0, keepdims=True) for d in range(3)], axis=0
-    )
-
-
-def gradients(table, pos, load, slope, vectors, all_atoms):
-    owned = pos.shape[1]
-    bm = 512
+    out = out - 0.5 * jnp.sum(sums["constant"], axis=1, keepdims=True)
+    out_ref[:8] = out[:8]
+    out_ref[8:12] = jnp.concatenate(
+        [jnp.sum(load * out[8 * d + 8 : 8 * d + 16], axis=0, keepdims=True) for d in range(3)]
+        + [jnp.sum(jnp.where(diagonal, energy, 0.0), axis=0, keepdims=True)],
+        axis=0,
+    )
+
+
+def gradients(table, atoms, slope, vectors, all_atoms):
+    owned = 2 * atoms.shape[2]
+    bm = 256
     return pl.pallas_call(
         functools.partial(gradient_kernel, all_atoms=all_atoms),
-        out_shape=(
-            jax.ShapeDtypeStruct((8, owned), F32),
-            jax.ShapeDtypeStruct((3, owned), F32),
-            jax.ShapeDtypeStruct((1, 8), F32),
-        ),
-        in_specs=[pl.BlockSpec(memory_space=pltpu.VMEM)] * 4,
-        out_specs=(pl.BlockSpec(memory_space=pltpu.VMEM),) * 3,
+        out_shape=jax.ShapeDtypeStruct((12, owned), F32),
+        in_specs=[pl.BlockSpec(memory_space=pltpu.VMEM)] * 3,
+        out_specs=pl.BlockSpec(memory_space=pltpu.VMEM),
         scratch_shapes=[
             pltpu.VMEM((32, vectors), BF16),
             pltpu.VMEM((64, vectors), BF16),
@@ -241,32 +266,60 @@
         ],
         compiler_params=pltpu.CompilerParams(vmem_limit_bytes=40 * 2**20),
         name="gradients",
-    )(table, pos, load, slope)
+    )(table, atoms, slope)
 
 
 def shards(pos, load, dual, weights, slope):
     owned = pos.shape[1] // lax.axis_size("k")
-    mine = lax.axis_index("k") * owned
-    own_pos = lax.dynamic_slice_in_dim(pos, mine, owned, 1)
-    own_load = lax.dynamic_slice_in_dim(load, mine, owned, 1)
     place = lax.axis_index(PLANE)
     vectors_here = jnp.concatenate([dual, weights[None]], axis=0)
-    own_vectors = lax.dynamic_slice(vectors_here, (place % 4, (place // 4) * 128), (1, 128))
+    group = (place % 2) * 4 + place // 8
+    own_vectors = lax.dynamic_slice(vectors_here, (place // 2 % 4, group * 128), (1, 128))
 
     partial = structure(pos, load, dual)
-    parts = lax.all_to_all(partial.reshape(32, 4, 128), PLANE, 0, 0, tiled=True)
+    parts = lax.all_to_all(
+        partial.reshape(32, 4, 128),
+        PLANE,
+        0,
+        0,
+        axis_index_groups=[[n ^ PLANE_FLIP for n in range(32)]],
+        tiled=True,
+    )
     block = jnp.concatenate([jnp.sum(parts, axis=0), own_vectors], axis=0)
-    column = lax.all_to_all(jnp.broadcast_to(block.reshape(640), (16, 640)), COLUMN, 0, 0, tiled=True)
-    column = column.reshape(2, 8, 5, 128)
+    column = lax.all_to_all(
+        jnp.broadcast_to(block.reshape(640), (16, 640)),
+        COLUMN,
+        0,
+        0,
+        axis_index_groups=[list(COLUMN_ORDER)],
+        tiled=True,
+    )
+    column = column.reshape(2, 8, 5, 128)[::-1]
     block = jnp.concatenate([column[0, :, :4] + column[1, :, :4], column[0, :, 4:]], axis=1)
     block = jnp.transpose(block, (1, 0, 2)).reshape(40, 128)
-    table = lax.all_to_all(jnp.broadcast_to(block, (32, 40, 128)), PLANE, 0, 0, tiled=True)
-    vectors = dual.shape[1] * lax.axis_size("k")
+
+    mine = lax.axis_index("k") * owned
+    atoms = jnp.concatenate(
+        [lax.dynamic_slice_in_dim(load, mine, owned, 1), lax.dynamic_slice_in_dim(pos, mine, owned, 1)], axis=0
+    )
+    atoms, slope, _ = lax.optimization_barrier((atoms, slope, column))
+    atoms = lax.all_gather(atoms, "c")
+    table = lax.all_to_all(
+        jnp.broadcast_to(block, (16, 40, 128)),
+        ("x", "y"),
+        0,
+        0,
+        axis_index_groups=[[n ^ CORE_PLANE_FLIP for n in range(16)]],
+        tiled=True,
+    )
+    vectors = dual.shape[1] * lax.axis_size("k") // 2
     all_atoms = pos.shape[1] * lax.axis_size(("zh",) + PLANE)
-    grad, force, energy = gradients(
-        table.reshape(1280, 128), own_pos, own_load, slope.reshape(8, 1), vectors, all_atoms
-    )
-    return grad, force, energy.reshape(8)
+    shares = lax.all_gather(
+        gradients(table.reshape(640, 128), atoms, slope.reshape(8, 1), vectors, all_atoms), "c"
+    )
+    sums = shares[0] + shares[1]
+    result = lax.dynamic_slice_in_dim(sums, lax.axis_index("c") * owned, owned, 1)
+    return result[:8], result[8:11], sums[11, :8]
 
 
 def solution(mesh):

time: 80.1 us -> 70.4 us (0.88)
  starting transfers between devices: 15.7 us -> 37.2 us
  blocking collectives: 24.3 us -> 5.42 us
  waiting for transfers between devices: 17.6 us -> 4.09 us
  local copies, waits for them, and re-layouts: 3.72 us -> 5.93 us
  Pallas kernels: 17.4 us -> 16.3 us
    all_to_all x1 -> x0, blocking collectives: 24.3 us -> none  [shards(): lax.all_to_all(jnp.broadcast_to(block.reshape(640), (16, 640)), COLUMN, 0...]
    all_to_all x2 -> x3, starting transfers between devices: 15.7 us -> 37.2 us  [the longest x1 14.8 us: shards(): lax.all_to_all(jnp.broadcast_to(block.reshape(640), (16, 640)), COLUMN, 0...]
    all_to_all x2 -> x3, waiting for transfers between devices: 17.6 us -> 4.09 us  [the longest x1 2.61 us: shards(): lax.all_to_all(jnp.broadcast_to(block.reshape(640), (16, 640)), COLUMN, 0...]
    all_gather x0 -> x2, blocking collectives: none -> 5.42 us  [the longest x1 3.47 us: shards(): atoms = lax.all_gather(atoms, 'c')]
    slice x0 -> x2, local copies, waits for them, and re-layouts: none -> 1.2 us  [shards(): return (result[:8], result[8:11], sums[11, :8])]
    pallas_call x1, Pallas kernels: 9.15 us -> 8.04 us  [gradients(): pl.pallas_call(functools.partial(gradient_kernel, all_atoms=all_atoms), o...]
  transfers between devices with their start and end apart: 2 -> 3, of which waited for: 2 -> 2; matrix products, arithmetic and copies ran while one was open for 2% -> 2% of each run, Pallas kernels for 0% -> 0%
where the time goes in v3:
time: 70.4 us; the launch traced here: 69.9 us
  starting transfers between devices  37.2 us (53%)
  Pallas kernels  16.3 us (23%)
  local copies, waits for them, and re-layouts  5.93 us (8%)
  blocking collectives  5.42 us (8%)
  waiting for transfers between devices  4.09 us (6%)
  between operations  0.76 us (1%)
    all_to_all x1, starting transfers between devices, shards(): lax.all_to_all(jnp.broadcast_to(block.reshape(640), (16, 640)), COLUMN, 0...  14.8 us
    all_to_all x1, starting transfers between devices, shards(): lax.all_to_all(partial.reshape(32, 4, 128), PLANE, 0, 0, axis_index_group...  13.9 us
    all_to_all x1, starting transfers between devices, shards(): lax.all_to_all(jnp.broadcast_to(block, (16, 40, 128)), ('x', 'y'), 0, 0,...  8.51 us
    pallas_call x1, Pallas kernels, structure(): pl.pallas_call(structure_kernel, out_shape=jax.ShapeDtypeStruct((vectors...  8.22 us
    pallas_call x1, Pallas kernels, gradients(): pl.pallas_call(functools.partial(gradient_kernel, all_atoms=all_atoms), o...  8.04 us
    all_gather x1, blocking collectives, shards(): atoms = lax.all_gather(atoms, 'c')  3.47 us
    all_to_all x1, waiting for transfers between devices, shards(): lax.all_to_all(jnp.broadcast_to(block.reshape(640), (16, 640)), COLUMN, 0...  2.61 us
    all_gather x1, blocking collectives, shards(): lax.all_gather(gradients(table.reshape(640, 128), atoms, slope.reshape(8,...  1.95 us
  transfers between devices with their start and end apart: 3, of which 2 were waited for; matrix products, arithmetic and copies ran while one was open for 2% of the time, Pallas kernels for 0%

profile of v3, /device:TPU:1, one launch (start us, length us, event | category | flops | bytes accessed | tf_op | source)
XLA Modules:
  0.0 69.9 jit_solution(6690000921278928492)
XLA Ops:
  0.6 8.2 %structure.1 = f32[128,128]{1,0:T(8,128)} custom-call(f32[3,2048]{1,0:T(4,128)} %pos_hbm.1, f32[8,2048]{1,0:T(8,128)} %load_hbm.1, f32[3,1024]{1,0:T(4,128)} %dual_hbm.1), custom_call_target="tpu_custom_call" | custom-call | tf_op jit(solution)/shard_map/structure/pallas_call | solution.py:136
  8.9 13.9 %all-to-all-start = ((f32[32,4,128]{2,1,0:T(4,128)}), f32[32,4,128]{2,1,0:T(4,128)S(1)}, u32[]{:S(2)}, u32[]{:S(2)}) async-start(f32[32,4,128]{2,1,0:T(4,128)} %bitcast.29), calls=%async_computation | async-start | bytes 131072 | tf_op jit(solution)/shard_map/all_to_all | solution.py:280
  22.8 0.0 copy-start
  22.8 0.0 copy-start.1
  22.9 0.7 copy-done
  23.5 0.0 copy-done.1
  23.5 0.1 fusion.1
  23.6 1.5 %all-to-all-done = f32[32,4,128]{2,1,0:T(4,128)S(1)} async-done(((f32[32,4,128]{2,1,0:T(4,128)}), f32[32,4,128]{2,1,0:T(4,128)S(1)}, u32[]{:S(2)}, u32[]{:S(2)}) %all-to-all-start) | async-done | bytes 65568 | tf_op jit(solution)/shard_map/all_to_all | solution.py:280
  25.2 0.6 broadcast_in_dim.13
  25.8 14.8 %all-to-all-start.1 = ((f32[16,1,640]{2,1,0:T(1,128)}), f32[16,1,640]{2,1,0:T(1,128)S(1)}, u32[]{:S(2)}, u32[]{:S(2)}) async-start(f32[16,1,640]{2,1,0:T(1,128)} %broadcast_in_dim.13), calls=%async_computation.1 | async-start | bytes 81920 | tf_op jit(solution)/shard_map/all_to_all | solution.py:289
  40.6 2.6 %all-to-all-done.1 = f32[16,1,640]{2,1,0:T(1,128)S(1)} async-done(((f32[16,1,640]{2,1,0:T(1,128)}), f32[16,1,640]{2,1,0:T(1,128)S(1)}, u32[]{:S(2)}, u32[]{:S(2)}) %all-to-all-start.1) | async-done | bytes 40992 | tf_op jit(solution)/shard_map/all_to_all | solution.py:289
  43.3 0.8 %broadcast_in_dim.14 = f32[16,40,128]{2,1,0:T(8,128)} broadcast(f32[40,128]{1,0:T(8,128)S(1)} %maximum_bitcast_fusion), dimensions={1,2} | broadcast | bytes 348160 | tf_op jit(solution)/shard_map/broadcast_in_dim | solution.py:308
  44.0 8.5 %all-to-all-start.2 = ((f32[16,40,128]{2,1,0:T(8,128)}), f32[16,40,128]{2,1,0:T(8,128)S(1)}, u32[]{:S(2)}, u32[]{:S(2)}) async-start(f32[16,40,128]{2,1,0:T(8,128)} %broadcast_in_dim.14), calls=%async_computation.2 | async-start | bytes 655360 | tf_op jit(solution)/shard_map/all_to_all | solution.py:307
  52.5 0.7 constant_dynamic-slice_fusion
  53.2 0.7 constant_dynamic-slice_fusion.1
  53.9 0.7 copy-done.2
  54.6 0.1 copy.11.slope_ref
  54.7 3.5 %all-gather.2.atoms_ref = f32[2,11,256]{2,1,0:T(8,128)S(1)} all-gather(f32[1,11,256]{2,1,0:T(8,128)S(1)} %bitcast.32), channel_id=2, replica_groups=mesh['zh'=2,'x'=4,'y'=4,'c'=2,'k'=8] {'c'}, dimensions={0}, use_global_device_ids=true | all-gather | bytes 33792 | tf_op jit(solution)/shard_map/all_gather | solution.py:306
  58.1 0.0 all-to-all-done.2
  58.1 8.0 %gradients.1 = f32[12,512]{1,0:T(8,128)S(1)} custom-call(f32[640,128]{1,0:T(8,128)S(1)} %bitcast.27, f32[2,11,256]{2,1,0:T(8,128)S(1)} %all-gather.2.atoms_ref, f32[8,1]{1,0:T(8,128)S(1)} %copy.11.slope_ref), custom_call_target="tpu_custom_call" | custom-call | tf_op jit(solution)/shard_map/gradients/pallas_call | solution.py:255
  66.2 2.0 %all-gather.3 = f32[2,12,512]{2,1,0:T(8,128)S(1)} all-gather(f32[1,12,512]{2,1,0:T(8,128)S(1)} %bitcast.28), channel_id=3, replica_groups=mesh['zh'=2,'x'=4,'y'=4,'c'=2,'k'=8] {'c'}, dimensions={0}, use_global_device_ids=true | all-gather | bytes 73728 | tf_op jit(solution)/shard_map/all_gather | solution.py:317
  68.1 0.6 dynamic-slice_bitcast_fusion
  68.8 0.6 dynamic-slice_bitcast_fusion.1
  69.3 0.5 slice_bitcast_fusion.1
  (10 shorter events, 0.1 us)
Async XLA Ops:
  8.9 16.2 %all-to-all-start = ((f32[32,4,128]{2,1,0:T(4,128)}), f32[32,4,128]{2,1,0:T(4,128)S(1)}, u32[]{:S(2)}, u32[]{:S(2)}) async-start(f32[32,4,128]{2,1,0:T(4,128)} %bitcast.29), calls=%async_computation | async-start | bytes 131072 | tf_op jit(solution)/shard_map/all_to_all | solution.py:280
  22.8 0.7 %copy-start = (f32[3,1024]{1,0:T(4,128)S(1)}, f32[3,1024]{1,0:T(4,128)}, u32[]{:S(2)}) copy-start(f32[3,1024]{1,0:T(4,128)} %dual_hbm.1) | copy-start | bytes 36868
  22.8 0.7 copy-start.1
  25.8 17.4 %all-to-all-start.1 = ((f32[16,1,640]{2,1,0:T(1,128)}), f32[16,1,640]{2,1,0:T(1,128)S(1)}, u32[]{:S(2)}, u32[]{:S(2)}) async-start(f32[16,1,640]{2,1,0:T(1,128)} %broadcast_in_dim.13), calls=%async_computation.1 | async-start | bytes 81920 | tf_op jit(solution)/shard_map/all_to_all | solution.py:289
  44.0 14.1 %all-to-all-start.2 = ((f32[16,40,128]{2,1,0:T(8,128)}), f32[16,40,128]{2,1,0:T(8,128)S(1)}, u32[]{:S(2)}, u32[]{:S(2)}) async-start(f32[16,40,128]{2,1,0:T(8,128)} %broadcast_in_dim.14), calls=%async_computation.2 | async-start | bytes 655360 | tf_op jit(solution)/shard_map/all_to_all | solution.py:307
  53.9 0.7 copy-start.2

commit v4 on v3

--- a/solution.py
+++ b/solution.py
@@ -81,14 +81,40 @@
     trig_weights(tiles - 1)
 
 
+def diagonal(width):
+    shape = (8, width)
+    return lax.broadcasted_iota(jnp.int32, shape, 0) == lax.broadcasted_iota(jnp.int32, shape, 1)
+
+
 def structure_kernel(
-    pos_hbm, load_hbm, dual_hbm, out_ref, pos_ref, load_ref, dual_ref, p_ref, q_ref, w_ref, turns_ref, trig_ref, sems
+    pos_hbm,
+    load_hbm,
+    dual_hbm,
+    weight_hbm,
+    slope_hbm,
+    out_ref,
+    own_atoms_ref,
+    pos_ref,
+    load_ref,
+    dual_ref,
+    weight_ref,
+    slope_ref,
+    p_ref,
+    q_ref,
+    w_ref,
+    turns_ref,
+    trig_ref,
+    sems,
 ):
+    pairs = (
+        (dual_hbm, dual_ref),
+        (pos_hbm, pos_ref),
+        (load_hbm, load_ref),
+        (weight_hbm, weight_ref),
+        (slope_hbm, slope_ref),
+    )
     copies = [
-        pltpu.make_async_copy(source, target, sems.at[n])
-        for n, (source, target) in enumerate(
-            ((dual_hbm, dual_ref), (pos_hbm, pos_ref), (load_hbm, load_ref))
-        )
+        pltpu.make_async_copy(source, target, sems.at[n]) for n, (source, target) in enumerate(pairs)
     ]
     for copy in copies:
         copy.start()
@@ -121,37 +147,56 @@
             factors = jnp.concatenate([real, imag], axis=0)
             for lane in range(0, bn, 128):
                 group = (j * bn + lane) // 128
-                for part in range(4):
-                    place = ((group % 4) * 8 + part * 2 + group // 4) ^ PLANE_FLIP
-                    out_ref[place * 4 : place * 4 + 4, :] = factors[
-                        part * 4 : part * 4 + 4, lane : lane + 128
-                    ]
+                for row in range(16):
+                    put(group, row // 4, row % 4, factors[row : row + 1, lane : lane + 128])
+
+    def put(group, part, row, value):
+        place = ((group % 4) * 8 + part * 2 + group // 4) ^ PLANE_FLIP
+        out_ref[place, :, row * 128 : (row + 1) * 128] = value
 
     pipelined(len(tiles), phase, weigh, turns_ref, trig_ref, 16)
 
-
-def structure(pos, load, dual):
+    copies[3].wait()
+    for group in range(vectors // 128):
+        lanes = slice(group * 128, (group + 1) * 128)
+        for part in range(3):
+            put(group, part, 4, dual_ref[part : part + 1, lanes])
+        put(group, 3, 4, weight_ref[:, lanes])
+    copies[4].wait()
+    owned = own_atoms_ref.shape[1]
+    mine = pl.ds(pl.multiple_of(lax.axis_index("k") * owned, 128), owned)
+    own_atoms_ref[:8] = load_ref[:, mine]
+    slope = jnp.concatenate([slope_ref[...], jnp.zeros((1, owned - 8), F32)], axis=1)
+    own_atoms_ref[8:12] = jnp.concatenate([pos_ref[:, mine], slope], axis=0)
+
+
+def structure(pos, load, dual, weights, slope, owned):
     atoms, vectors = pos.shape[1], dual.shape[1]
     bm, bn = 512, 256
     return pl.pallas_call(
         structure_kernel,
-        out_shape=jax.ShapeDtypeStruct((vectors // 8, 128), F32),
-        in_specs=[pl.BlockSpec(memory_space=pl.ANY)] * 3,
-        out_specs=pl.BlockSpec(memory_space=pltpu.VMEM),
+        out_shape=(
+            pltpu.VMEM((32, 1, 640), F32),
+            pltpu.VMEM((12, owned), F32),
+        ),
+        in_specs=[pl.BlockSpec(memory_space=pl.ANY)] * 5,
+        out_specs=(pl.BlockSpec(memory_space=pltpu.VMEM),) * 2,
         scratch_shapes=[
             pltpu.VMEM(pos.shape, F32),
             pltpu.VMEM(load.shape, F32),
             pltpu.VMEM(dual.shape, F32),
+            pltpu.VMEM(weights.shape, F32),
+            pltpu.VMEM(slope.shape, F32),
             pltpu.VMEM((32, atoms), BF16),
             pltpu.VMEM((32, vectors), BF16),
             pltpu.VMEM((16, atoms), BF16),
             pltpu.VMEM((2, bm, bn), F32),
             pltpu.VMEM((2, 4, bm, bn), BF16),
-            pltpu.SemaphoreType.DMA((3,)),
+            pltpu.SemaphoreType.DMA((5,)),
         ],
         compiler_params=pltpu.CompilerParams(vmem_limit_bytes=60 * 2**20),
         name="structure",
-    )(pos, load, dual)
+    )(pos, load, dual, weights, slope)
 
 
 def spread_four(value, outer):
@@ -171,7 +216,6 @@
 def gradient_kernel(
     table_ref,
     atoms_ref,
-    slope_ref,
     out_ref,
     p_ref,
     versine_ref,
@@ -187,7 +231,7 @@
     load = atoms[:8]
     pos = jnp.concatenate([atoms[8:11] - CENTRE, jnp.zeros((1, owned), F32)], axis=0)
     q = spread_four(pos, False)
-    slope = 4.0 * slope_ref[...]
+    slope = 4.0 * jnp.sum(jnp.where(diagonal(128), atoms_ref[0, 11:12, :128], 0.0), axis=1, keepdims=True)
     is_dual = lax.broadcasted_iota(jnp.int32, (4, 128), 0) < 3
     sums = {
         "energy": jnp.zeros((8, 128), F32),
@@ -237,25 +281,23 @@
 
     pipelined(vectors // bm, phase, weigh, turns_ref, trig_ref, 16)
     energy = jnp.sum(sums["energy"], axis=1, keepdims=True) * (1.0 / all_atoms)
-    shape = (8, owned)
-    diagonal = lax.broadcasted_iota(jnp.int32, shape, 0) == lax.broadcasted_iota(jnp.int32, shape, 1)
     out = sums["high"][:32] + sums["high"][32:] + sums["low"]
     out = out - 0.5 * jnp.sum(sums["constant"], axis=1, keepdims=True)
     out_ref[:8] = out[:8]
     out_ref[8:12] = jnp.concatenate(
         [jnp.sum(load * out[8 * d + 8 : 8 * d + 16], axis=0, keepdims=True) for d in range(3)]
-        + [jnp.sum(jnp.where(diagonal, energy, 0.0), axis=0, keepdims=True)],
+        + [jnp.sum(jnp.where(diagonal(owned), energy, 0.0), axis=0, keepdims=True)],
         axis=0,
     )
 
 
-def gradients(table, atoms, slope, vectors, all_atoms):
+def gradients(table, atoms, vectors, all_atoms):
     owned = 2 * atoms.shape[2]
     bm = 256
     return pl.pallas_call(
         functools.partial(gradient_kernel, all_atoms=all_atoms),
-        out_shape=jax.ShapeDtypeStruct((12, owned), F32),
-        in_specs=[pl.BlockSpec(memory_space=pltpu.VMEM)] * 3,
+        out_shape=pltpu.VMEM((12, owned), F32),
+        in_specs=[pl.BlockSpec(memory_space=pltpu.VMEM)] * 2,
         out_specs=pl.BlockSpec(memory_space=pltpu.VMEM),
         scratch_shapes=[
             pltpu.VMEM((32, vectors), BF16),
@@ -266,44 +308,60 @@
         ],
         compiler_params=pltpu.CompilerParams(vmem_limit_bytes=40 * 2**20),
         name="gradients",
-    )(table, atoms, slope)
+    )(table, atoms)
+
+
+def finish_kernel(shares_ref, grad_ref, force_ref, energy_ref):
+    owned = grad_ref.shape[1]
+    mine = pl.ds(pl.multiple_of(lax.axis_index("c") * owned, 128), owned)
+    grad_ref[...] = shares_ref[0, :8, mine] + shares_ref[1, :8, mine]
+    force_ref[...] = shares_ref[0, 8:11, mine] + shares_ref[1, 8:11, mine]
+    energy_ref[...] = shares_ref[0, 11:12, :8] + shares_ref[1, 11:12, :8]
+
+
+def finish(shares):
+    owned = shares.shape[2] // 2
+    return pl.pallas_call(
+        finish_kernel,
+        out_shape=(
+            jax.ShapeDtypeStruct((8, owned), F32),
+            jax.ShapeDtypeStruct((3, owned), F32),
+            jax.ShapeDtypeStruct((1, 8), F32),
+        ),
+        in_specs=[pl.BlockSpec(memory_space=pltpu.VMEM)],
+        out_specs=(pl.BlockSpec(memory_space=pltpu.VMEM),) * 3,
+        name="finish",
+    )(shares)
 
 
 def shards(pos, load, dual, weights, slope):
     owned = pos.shape[1] // lax.axis_size("k")
-    place = lax.axis_index(PLANE)
-    vectors_here = jnp.concatenate([dual, weights[None]], axis=0)
-    group = (place % 2) * 4 + place // 8
-    own_vectors = lax.dynamic_slice(vectors_here, (place // 2 % 4, group * 128), (1, 128))
-
-    partial = structure(pos, load, dual)
+    partial, atoms = structure(
+        pos, load, dual, weights.reshape(1, -1), slope.reshape(1, -1), owned
+    )
     parts = lax.all_to_all(
-        partial.reshape(32, 4, 128),
+        partial,
         PLANE,
         0,
         0,
         axis_index_groups=[[n ^ PLANE_FLIP for n in range(32)]],
         tiled=True,
     )
-    block = jnp.concatenate([jnp.sum(parts, axis=0), own_vectors], axis=0)
+    block = jnp.concatenate([jnp.sum(parts[:, :, :512], axis=0), parts[0, :, 512:]], axis=1)
+    atoms, block = lax.optimization_barrier((atoms, block))
+    atoms = lax.all_gather(atoms, "c")
     column = lax.all_to_all(
-        jnp.broadcast_to(block.reshape(640), (16, 640)),
+        jnp.broadcast_to(block, (16, 1, 640)),
         COLUMN,
         0,
         0,
         axis_index_groups=[list(COLUMN_ORDER)],
         tiled=True,
     )
-    column = column.reshape(2, 8, 5, 128)[::-1]
-    block = jnp.concatenate([column[0, :, :4] + column[1, :, :4], column[0, :, 4:]], axis=1)
+    atoms, column = lax.optimization_barrier((atoms, column))
+    column = column.reshape(2, 8, 5, 128)
+    block = jnp.concatenate([column[1, :, :4] + column[0, :, :4], column[0, :, 4:]], axis=1)
     block = jnp.transpose(block, (1, 0, 2)).reshape(40, 128)
-
-    mine = lax.axis_index("k") * owned
-    atoms = jnp.concatenate(
-        [lax.dynamic_slice_in_dim(load, mine, owned, 1), lax.dynamic_slice_in_dim(pos, mine, owned, 1)], axis=0
-    )
-    atoms, slope, _ = lax.optimization_barrier((atoms, slope, column))
-    atoms = lax.all_gather(atoms, "c")
     table = lax.all_to_all(
         jnp.broadcast_to(block, (16, 40, 128)),
         ("x", "y"),
@@ -314,12 +372,9 @@
     )
     vectors = dual.shape[1] * lax.axis_size("k") // 2
     all_atoms = pos.shape[1] * lax.axis_size(("zh",) + PLANE)
-    shares = lax.all_gather(
-        gradients(table.reshape(640, 128), atoms, slope.reshape(8, 1), vectors, all_atoms), "c"
-    )
-    sums = shares[0] + shares[1]
-    result = lax.dynamic_slice_in_dim(sums, lax.axis_index("c") * owned, owned, 1)
-    return result[:8], result[8:11], sums[11, :8]
+    shares = lax.all_gather(gradients(table.reshape(640, 128), atoms, vectors, all_atoms), "c")
+    grad, force, energy = finish(shares)
+    return grad, force, energy.reshape(8)
 
 
 def solution(mesh):

time: 70.4 us -> 67.7 us (0.962)
  blocking collectives: 5.42 us -> 34.2 us
  starting transfers between devices: 37.2 us -> 14.6 us
  local copies, waits for them, and re-layouts: 5.93 us -> 0.67 us
  waiting for transfers between devices: 4.09 us -> 0.01 us
  Pallas kernels: 16.3 us -> 17.1 us
    all_to_all x0 -> x2, blocking collectives: none -> 27.1 us  [the longest x1 16.1 us: shards(): lax.all_to_all(partial, PLANE, 0, 0, axis_index_groups=[[n ^ PLANE_FLIP f...]
    all_to_all x3 -> x1, starting transfers between devices: 37.2 us -> 14.6 us  [shards(): lax.all_to_all(jnp.broadcast_to(block, (16, 1, 640)), COLUMN, 0, 0, axis_...]
    all_to_all x3 -> x1, waiting for transfers between devices: 4.09 us -> 0.01 us  [shards(): lax.all_to_all(jnp.broadcast_to(block, (16, 1, 640)), COLUMN, 0, 0, axis_...]
    all_gather x1, blocking collectives: 1.95 us -> 4.49 us  [shards(): lax.all_gather(gradients(table.reshape(640, 128), atoms, vectors, all_ato...]
    dynamic_slice x2 -> x0, local copies, waits for them, and re-layouts: 1.38 us -> none  [the longest x1 0.7 us: shards(): lax.dynamic_slice_in_dim(load, mine, owned, 1)]
    unnamed x6 -> x0, local copies, waits for them, and re-layouts: 1.34 us -> none
    slice x2 -> x0, local copies, waits for them, and re-layouts: 1.2 us -> none  [shards(): return (result[:8], result[8:11], sums[11, :8])]
    pallas_call x1 -> x2, Pallas kernels: 8.22 us -> 9.11 us  [the longest x1 7.67 us: structure(): pl.pallas_call(structure_kernel, out_shape=(pltpu.VMEM((32, 1, 640), F32)...]
  transfers between devices with their start and end apart: 3 -> 1, of which waited for: 2 -> 0; matrix products, arithmetic and copies ran while one was open for 2% -> 0% of each run, Pallas kernels for 0% -> 0%
where the time goes in v4:
time: 67.7 us; the launch traced here: 67.4 us
  blocking collectives  34.2 us (51%)
  Pallas kernels  17.1 us (25%)
  starting transfers between devices  14.6 us (22%)
  between operations  0.68 us (1%)
    all_to_all x1, blocking collectives, shards(): lax.all_to_all(partial, PLANE, 0, 0, axis_index_groups=[[n ^ PLANE_FLIP f...  16.1 us
    all_to_all x1, starting transfers between devices, shards(): lax.all_to_all(jnp.broadcast_to(block, (16, 1, 640)), COLUMN, 0, 0, axis_...  14.6 us
    all_to_all x1, blocking collectives, shards(): lax.all_to_all(jnp.broadcast_to(block, (16, 40, 128)), ('x', 'y'), 0, 0,...  11 us
    pallas_call x1, Pallas kernels, gradients(): pl.pallas_call(functools.partial(gradient_kernel, all_atoms=all_atoms), o...  8.03 us
    pallas_call x1, Pallas kernels, structure(): pl.pallas_call(structure_kernel, out_shape=(pltpu.VMEM((32, 1, 640), F32)...  7.67 us
    all_gather x1, blocking collectives, shards(): lax.all_gather(gradients(table.reshape(640, 128), atoms, vectors, all_ato...  4.49 us
    all_gather x1, blocking collectives, shards(): atoms = lax.all_gather(atoms, 'c')  2.66 us
    pallas_call x1, Pallas kernels, finish(): pl.pallas_call(finish_kernel, out_shape=(jax.ShapeDtypeStruct((8, owned),...  1.45 us
  transfers between devices with their start and end apart: 1, of which 0 were waited for; matrix products, arithmetic and copies ran while one was open for 0% of the time, Pallas kernels for 0%

profile of v4, /device:TPU:1, one launch (start us, length us, event | category | flops | bytes accessed | tf_op | source)
XLA Modules:
  0.0 67.4 jit_solution(5500101104342368088)
XLA Ops:
  0.6 7.7 %structure.1 = (f32[32,1,640]{2,1,0:T(1,128)S(1)}, f32[12,256]{1,0:T(8,128)S(1)}) custom-call(f32[3,2048]{1,0:T(4,128)} %pos_hbm.1, f32[8,2048]{1,0:T(8,128)} %load_hbm.1, f32[3,1024]{1,0:T(4,128)} %dual_hbm.1, f32[1,1024]{1,0:T(1,128)} %bitcast.26, f32[1,8]{1,0:T(1,128)} %bitcast.27), custom_call_target="tpu_custom_call" | custom-call | tf_op jit(solution)/shard_map/structure/pallas_call | solution.py:176
  8.3 16.1 %all_to_all.15 = f32[32,1,640]{2,1,0:T(1,128)S(1)} all-to-all(f32[32,1,640]{2,1,0:T(1,128)S(1)} %get-tuple-element.13), channel_id=1, replica_groups={{160,168,176,184,128,136,144,152,224,232,240,248,192,200,208,216,32,40,..., dimensions={0} | all-to-all | bytes 163840 | tf_op jit(solution)/shard_map/all_to_all | solution.py:342
  24.4 0.1 slice_reduce_fusion
  24.5 0.6 broadcast_in_dim.6
  25.1 14.6 %all-to-all-start.1 = ((f32[16,1,640]{2,1,0:T(1,128)}), f32[16,1,640]{2,1,0:T(1,128)S(1)}, u32[]{:S(2)}, u32[]{:S(2)}) async-start(f32[16,1,640]{2,1,0:T(1,128)} %broadcast_in_dim.6), calls=%async_computation.1 | async-start | bytes 81920 | tf_op jit(solution)/shard_map/all_to_all | solution.py:353
  39.7 2.7 %all-gather.2.atoms_ref = f32[2,12,256]{2,1,0:T(8,128)S(1)} all-gather(f32[1,12,256]{2,1,0:T(8,128)S(1)} %bitcast.22), channel_id=2, replica_groups=mesh['zh'=2,'x'=4,'y'=4,'c'=2,'k'=8] {'c'}, dimensions={0}, use_global_device_ids=true | all-gather | bytes 36864 | tf_op jit(solution)/shard_map/all_gather | solution.py:352
  42.3 0.0 all-to-all-done.1
  42.4 11.0 %all_to_all.16 = f32[16,40,128]{2,1,0:T(8,128)S(1)} all-to-all(f32[16,40,128]{2,1,0:T(8,128)S(1)} %broadcast_in_dim.7), channel_id=1, replica_groups={{160,176,128,144,224,240,192,208,32,48,0,16,96,112,64,80},{161,177,129,..., dimensions={0} | all-to-all | bytes 655360 | tf_op jit(solution)/shard_map/all_to_all | solution.py:365
  53.4 8.0 %gradients.1 = f32[12,512]{1,0:T(8,128)S(1)} custom-call(f32[640,128]{1,0:T(8,128)S(1)} %bitcast.20, f32[2,12,256]{2,1,0:T(8,128)S(1)} %all-gather.2.atoms_ref), custom_call_target="tpu_custom_call" | custom-call | tf_op jit(solution)/shard_map/gradients/pallas_call | solution.py:297
  61.4 4.5 %all-gather.3.shares_ref = f32[2,12,512]{2,1,0:T(8,128)} all-gather(f32[1,12,512]{2,1,0:T(8,128)S(1)} %bitcast.21), channel_id=3, replica_groups=mesh['zh'=2,'x'=4,'y'=4,'c'=2,'k'=8] {'c'}, dimensions={0}, use_global_device_ids=true | all-gather | bytes 73728 | tf_op jit(solution)/shard_map/all_gather | solution.py:375
  65.9 1.4 %finish.1 = (f32[8,256]{1,0:T(8,128)}, f32[3,256]{1,0:T(4,128)}, f32[1,8]{1,0:T(1,128)}) custom-call(f32[2,12,512]{2,1,0:T(8,128)} %all-gather.3.shares_ref), custom_call_target="tpu_custom_call" | custom-call | tf_op jit(solution)/shard_map/finish/pallas_call | solution.py:324
  (8 shorter events, 0.1 us)
Async XLA Ops:
  25.1 17.2 %all-to-all-start.1 = ((f32[16,1,640]{2,1,0:T(1,128)}), f32[16,1,640]{2,1,0:T(1,128)S(1)}, u32[]{:S(2)}, u32[]{:S(2)}) async-start(f32[16,1,640]{2,1,0:T(1,128)} %broadcast_in_dim.6), calls=%async_computation.1 | async-start | bytes 81920 | tf_op jit(solution)/shard_map/all_to_all | solution.py:353

commit v5 on v4

--- a/solution.py
+++ b/solution.py
@@ -13,8 +13,8 @@
 F32 = jnp.float32
 PLANE = ("x", "y", "c")
 COLUMN = ("zh", "k")
-PLANE_FLIP = 20
-CORE_PLANE_FLIP = 10
+PLANE_ORDER = sorted(range(32), key=lambda p: (abs(p // 8 - 2) + abs(p // 2 % 4 - 2), p ^ 1))
+CORE_PLANE_ORDER = sorted(range(16), key=lambda p: abs(p // 4 - 2) + abs(p % 4 - 2))
 COLUMN_ORDER = (*range(8, 16), *range(8))
 CENTRE = 70.0
 SINE = (2.2214303016662598, -0.9131746292114258, 0.10983827710151672)
@@ -151,7 +151,7 @@
                     put(group, row // 4, row % 4, factors[row : row + 1, lane : lane + 128])
 
     def put(group, part, row, value):
-        place = ((group % 4) * 8 + part * 2 + group // 4) ^ PLANE_FLIP
+        place = PLANE_ORDER.index((group % 4) * 8 + part * 2 + group // 4)
         out_ref[place, :, row * 128 : (row + 1) * 128] = value
 
     pipelined(len(tiles), phase, weigh, turns_ref, trig_ref, 16)
@@ -241,13 +241,13 @@
     }
 
     def duals(b):
-        places = [((b // 8) * 4 + part) ^ CORE_PLANE_FLIP for part in range(4)]
+        places = [CORE_PLANE_ORDER.index((b // 8) * 4 + part) for part in range(4)]
         return jnp.concatenate([table_ref[pl.ds(at * 40 + 32 + b % 8, 1), :] for at in places], axis=0)
 
     def weights(b):
         g, zl = b // 8, b % 8
         rows = [
-            table_ref[pl.ds(((g * 4 + part) ^ CORE_PLANE_FLIP) * 40 + zl, 4, stride=8), :]
+            table_ref[pl.ds(CORE_PLANE_ORDER.index(g * 4 + part) * 40 + zl, 4, stride=8), :]
             for part in range(4)
         ]
         dual = duals(b)
@@ -344,7 +344,7 @@
         PLANE,
         0,
         0,
-        axis_index_groups=[[n ^ PLANE_FLIP for n in range(32)]],
+        axis_index_groups=[PLANE_ORDER],
         tiled=True,
     )
     block = jnp.concatenate([jnp.sum(parts[:, :, :512], axis=0), parts[0, :, 512:]], axis=1)
@@ -367,7 +367,7 @@
         ("x", "y"),
         0,
         0,
-        axis_index_groups=[[n ^ CORE_PLANE_FLIP for n in range(16)]],
+        axis_index_groups=[CORE_PLANE_ORDER],
         tiled=True,
     )
     vectors = dual.shape[1] * lax.axis_size("k") // 2

time: 67.7 us -> 67.2 us (level)
  transfers between devices with their start and end apart: 1 -> 1, of which waited for: 0 -> 1; matrix products, arithmetic and copies ran while one was open for 0% -> 0% of each run, Pallas kernels for 0% -> 0%
where the time goes in v5:
time: 67.2 us; the launch traced here: 66.9 us
  blocking collectives  33.6 us (50%)
  Pallas kernels  17.1 us (25%)
  starting transfers between devices  14.6 us (22%)
    all_to_all x1, blocking collectives, shards(): lax.all_to_all(partial, PLANE, 0, 0, axis_index_groups=[PLANE_ORDER], til...  15.9 us
    all_to_all x1, starting transfers between devices, shards(): lax.all_to_all(jnp.broadcast_to(block, (16, 1, 640)), COLUMN, 0, 0, axis_...  14.6 us
    all_to_all x1, blocking collectives, shards(): lax.all_to_all(jnp.broadcast_to(block, (16, 40, 128)), ('x', 'y'), 0, 0,...  10.7 us
    pallas_call x1, Pallas kernels, gradients(): pl.pallas_call(functools.partial(gradient_kernel, all_atoms=all_atoms), o...  8.03 us
    pallas_call x1, Pallas kernels, structure(): pl.pallas_call(structure_kernel, out_shape=(pltpu.VMEM((32, 1, 640), F32)...  7.67 us
    all_gather x1, blocking collectives, shards(): lax.all_gather(gradients(table.reshape(640, 128), atoms, vectors, all_ato...  4.49 us
    all_gather x1, blocking collectives, shards(): atoms = lax.all_gather(atoms, 'c')  2.43 us
    pallas_call x1, Pallas kernels, finish(): pl.pallas_call(finish_kernel, out_shape=(jax.ShapeDtypeStruct((8, owned),...  1.45 us
  transfers between devices with their start and end apart: 1, of which 1 were waited for; matrix products, arithmetic and copies ran while one was open for 0% of the time, Pallas kernels for 0%

profile of v5, /device:TPU:1, one launch (start us, length us, event | category | flops | bytes accessed | tf_op | source)
XLA Modules:
  0.0 66.9 jit_solution(3647570635520177110)
XLA Ops:
  0.6 7.7 %structure.1 = (f32[32,1,640]{2,1,0:T(1,128)S(1)}, f32[12,256]{1,0:T(8,128)S(1)}) custom-call(f32[3,2048]{1,0:T(4,128)} %pos_hbm.1, f32[8,2048]{1,0:T(8,128)} %load_hbm.1, f32[3,1024]{1,0:T(4,128)} %dual_hbm.1, f32[1,1024]{1,0:T(1,128)} %bitcast.26, f32[1,8]{1,0:T(1,128)} %bitcast.27), custom_call_target="tpu_custom_call" | custom-call | tf_op jit(solution)/shard_map/structure/pallas_call | solution.py:176
  8.3 15.9 %all_to_all.15 = f32[32,1,640]{2,1,0:T(1,128)S(1)} all-to-all(f32[32,1,640]{2,1,0:T(1,128)S(1)} %get-tuple-element.13), channel_id=1, replica_groups={{168,160,104,96,152,144,184,176,232,224,40,32,88,80,120,112,136,128,216..., dimensions={0} | all-to-all | bytes 163840 | tf_op jit(solution)/shard_map/all_to_all | solution.py:342
  24.3 0.1 slice_reduce_fusion
  24.3 0.6 broadcast_in_dim.6
  25.0 14.6 %all-to-all-start.1 = ((f32[16,1,640]{2,1,0:T(1,128)}), f32[16,1,640]{2,1,0:T(1,128)S(1)}, u32[]{:S(2)}, u32[]{:S(2)}) async-start(f32[16,1,640]{2,1,0:T(1,128)} %broadcast_in_dim.6), calls=%async_computation.1 | async-start | bytes 81920 | tf_op jit(solution)/shard_map/all_to_all | solution.py:353
  39.5 2.4 %all-gather.2.atoms_ref = f32[2,12,256]{2,1,0:T(8,128)S(1)} all-gather(f32[1,12,256]{2,1,0:T(8,128)S(1)} %bitcast.22), channel_id=2, replica_groups=mesh['zh'=2,'x'=4,'y'=4,'c'=2,'k'=8] {'c'}, dimensions={0}, use_global_device_ids=true | all-gather | bytes 36864 | tf_op jit(solution)/shard_map/all_gather | solution.py:352
  42.0 0.2 all-to-all-done.1
  42.2 10.7 %all_to_all.16 = f32[16,40,128]{2,1,0:T(8,128)S(1)} all-to-all(f32[16,40,128]{2,1,0:T(8,128)S(1)} %broadcast_in_dim.7), channel_id=1, replica_groups={{160,96,144,176,224,32,80,112,128,208,240,16,48,64,192,0},{161,97,145,1..., dimensions={0} | all-to-all | bytes 655360 | tf_op jit(solution)/shard_map/all_to_all | solution.py:365
  52.9 8.0 %gradients.1 = f32[12,512]{1,0:T(8,128)S(1)} custom-call(f32[640,128]{1,0:T(8,128)S(1)} %bitcast.20, f32[2,12,256]{2,1,0:T(8,128)S(1)} %all-gather.2.atoms_ref), custom_call_target="tpu_custom_call" | custom-call | tf_op jit(solution)/shard_map/gradients/pallas_call | solution.py:297
  60.9 4.5 %all-gather.3.shares_ref = f32[2,12,512]{2,1,0:T(8,128)} all-gather(f32[1,12,512]{2,1,0:T(8,128)S(1)} %bitcast.21), channel_id=3, replica_groups=mesh['zh'=2,'x'=4,'y'=4,'c'=2,'k'=8] {'c'}, dimensions={0}, use_global_device_ids=true | all-gather | bytes 73728 | tf_op jit(solution)/shard_map/all_gather | solution.py:375
  65.4 1.4 %finish.1 = (f32[8,256]{1,0:T(8,128)}, f32[3,256]{1,0:T(4,128)}, f32[1,8]{1,0:T(1,128)}) custom-call(f32[2,12,512]{2,1,0:T(8,128)} %all-gather.3.shares_ref), custom_call_target="tpu_custom_call" | custom-call | tf_op jit(solution)/shard_map/finish/pallas_call | solution.py:324
  (8 shorter events, 0.1 us)
Async XLA Ops:
  25.0 17.2 %all-to-all-start.1 = ((f32[16,1,640]{2,1,0:T(1,128)}), f32[16,1,640]{2,1,0:T(1,128)S(1)}, u32[]{:S(2)}, u32[]{:S(2)}) async-start(f32[16,1,640]{2,1,0:T(1,128)} %broadcast_in_dim.6), calls=%async_computation.1 | async-start | bytes 81920 | tf_op jit(solution)/shard_map/all_to_all | solution.py:353

commit v6 on v5

--- a/solution.py
+++ b/solution.py
@@ -137,6 +137,8 @@
 
     def weigh(t):
         i, j = tiles[t]
+        if t == 1:
+            hand_out()
         w = w_ref[:, i * bm : (i + 1) * bm]
         for part in range(4):
             term = product(w, trig_ref[t % 2, part])
@@ -154,20 +156,21 @@
         place = PLANE_ORDER.index((group % 4) * 8 + part * 2 + group // 4)
         out_ref[place, :, row * 128 : (row + 1) * 128] = value
 
+    def hand_out():
+        copies[3].wait()
+        for group in range(vectors // 128):
+            lanes = slice(group * 128, (group + 1) * 128)
+            for part in range(3):
+                put(group, part, 4, dual_ref[part : part + 1, lanes])
+            put(group, 3, 4, weight_ref[:, lanes])
+        copies[4].wait()
+        owned = own_atoms_ref.shape[1]
+        mine = pl.ds(pl.multiple_of(lax.axis_index("k") * owned, 128), owned)
+        own_atoms_ref[:8] = load_ref[:, mine]
+        slope = jnp.concatenate([slope_ref[...], jnp.zeros((1, owned - 8), F32)], axis=1)
+        own_atoms_ref[8:12] = jnp.concatenate([pos_ref[:, mine], slope], axis=0)
+
     pipelined(len(tiles), phase, weigh, turns_ref, trig_ref, 16)
-
-    copies[3].wait()
-    for group in range(vectors // 128):
-        lanes = slice(group * 128, (group + 1) * 128)
-        for part in range(3):
-            put(group, part, 4, dual_ref[part : part + 1, lanes])
-        put(group, 3, 4, weight_ref[:, lanes])
-    copies[4].wait()
-    owned = own_atoms_ref.shape[1]
-    mine = pl.ds(pl.multiple_of(lax.axis_index("k") * owned, 128), owned)
-    own_atoms_ref[:8] = load_ref[:, mine]
-    slope = jnp.concatenate([slope_ref[...], jnp.zeros((1, owned - 8), F32)], axis=1)
-    own_atoms_ref[8:12] = jnp.concatenate([pos_ref[:, mine], slope], axis=0)
 
 
 def structure(pos, load, dual, weights, slope, owned):

time: 67.2 us -> 67.4 us (level)
  no operation moved by 1% of the time
where the time goes in v6:
time: 67.4 us; the launch traced here: 67.1 us
  blocking collectives  33.6 us (50%)
  Pallas kernels  17.4 us (26%)
  starting transfers between devices  14.6 us (22%)
    all_to_all x1, blocking collectives, shards(): lax.all_to_all(partial, PLANE, 0, 0, axis_index_groups=[PLANE_ORDER], til...  15.9 us
    all_to_all x1, starting transfers between devices, shards(): lax.all_to_all(jnp.broadcast_to(block, (16, 1, 640)), COLUMN, 0, 0, axis_...  14.6 us
    all_to_all x1, blocking collectives, shards(): lax.all_to_all(jnp.broadcast_to(block, (16, 40, 128)), ('x', 'y'), 0, 0,...  10.7 us
    pallas_call x1, Pallas kernels, gradients(): pl.pallas_call(functools.partial(gradient_kernel, all_atoms=all_atoms), o...  8.03 us
    pallas_call x1, Pallas kernels, structure(): pl.pallas_call(structure_kernel, out_shape=(pltpu.VMEM((32, 1, 640), F32)...  7.89 us
    all_gather x1, blocking collectives, shards(): lax.all_gather(gradients(table.reshape(640, 128), atoms, vectors, all_ato...  4.49 us
    all_gather x1, blocking collectives, shards(): atoms = lax.all_gather(atoms, 'c')  2.43 us
    pallas_call x1, Pallas kernels, finish(): pl.pallas_call(finish_kernel, out_shape=(jax.ShapeDtypeStruct((8, owned),...  1.45 us
  transfers between devices with their start and end apart: 1, of which 1 were waited for; matrix products, arithmetic and copies ran while one was open for 0% of the time, Pallas kernels for 0%

profile of v6, /device:TPU:1, one launch (start us, length us, event | category | flops | bytes accessed | tf_op | source)
XLA Modules:
  0.0 67.1 jit_solution(5646788138470584314)
XLA Ops:
  0.6 7.9 %structure.1 = (f32[32,1,640]{2,1,0:T(1,128)S(1)}, f32[12,256]{1,0:T(8,128)S(1)}) custom-call(f32[3,2048]{1,0:T(4,128)} %pos_hbm.1, f32[8,2048]{1,0:T(8,128)} %load_hbm.1, f32[3,1024]{1,0:T(4,128)} %dual_hbm.1, f32[1,1024]{1,0:T(1,128)} %bitcast.26, f32[1,8]{1,0:T(1,128)} %bitcast.27), custom_call_target="tpu_custom_call" | custom-call | tf_op jit(solution)/shard_map/structure/pallas_call | solution.py:179
  8.5 15.9 %all_to_all.15 = f32[32,1,640]{2,1,0:T(1,128)S(1)} all-to-all(f32[32,1,640]{2,1,0:T(1,128)S(1)} %get-tuple-element.13), channel_id=1, replica_groups={{168,160,104,96,152,144,184,176,232,224,40,32,88,80,120,112,136,128,216..., dimensions={0} | all-to-all | bytes 163840 | tf_op jit(solution)/shard_map/all_to_all | solution.py:345
  24.5 0.1 slice_reduce_fusion
  24.6 0.6 broadcast_in_dim.6
  25.2 14.6 %all-to-all-start.1 = ((f32[16,1,640]{2,1,0:T(1,128)}), f32[16,1,640]{2,1,0:T(1,128)S(1)}, u32[]{:S(2)}, u32[]{:S(2)}) async-start(f32[16,1,640]{2,1,0:T(1,128)} %broadcast_in_dim.6), calls=%async_computation.1 | async-start | bytes 81920 | tf_op jit(solution)/shard_map/all_to_all | solution.py:356
  39.8 2.4 %all-gather.2.atoms_ref = f32[2,12,256]{2,1,0:T(8,128)S(1)} all-gather(f32[1,12,256]{2,1,0:T(8,128)S(1)} %bitcast.22), channel_id=2, replica_groups=mesh['zh'=2,'x'=4,'y'=4,'c'=2,'k'=8] {'c'}, dimensions={0}, use_global_device_ids=true | all-gather | bytes 36864 | tf_op jit(solution)/shard_map/all_gather | solution.py:355
  42.2 0.2 all-to-all-done.1
  42.4 10.7 %all_to_all.16 = f32[16,40,128]{2,1,0:T(8,128)S(1)} all-to-all(f32[16,40,128]{2,1,0:T(8,128)S(1)} %broadcast_in_dim.7), channel_id=1, replica_groups={{160,96,144,176,224,32,80,112,128,208,240,16,48,64,192,0},{161,97,145,1..., dimensions={0} | all-to-all | bytes 655360 | tf_op jit(solution)/shard_map/all_to_all | solution.py:368
  53.1 8.0 %gradients.1 = f32[12,512]{1,0:T(8,128)S(1)} custom-call(f32[640,128]{1,0:T(8,128)S(1)} %bitcast.20, f32[2,12,256]{2,1,0:T(8,128)S(1)} %all-gather.2.atoms_ref), custom_call_target="tpu_custom_call" | custom-call | tf_op jit(solution)/shard_map/gradients/pallas_call | solution.py:300
  61.2 4.5 %all-gather.3.shares_ref = f32[2,12,512]{2,1,0:T(8,128)} all-gather(f32[1,12,512]{2,1,0:T(8,128)S(1)} %bitcast.21), channel_id=3, replica_groups=mesh['zh'=2,'x'=4,'y'=4,'c'=2,'k'=8] {'c'}, dimensions={0}, use_global_device_ids=true | all-gather | bytes 73728 | tf_op jit(solution)/shard_map/all_gather | solution.py:378
  65.7 1.4 %finish.1 = (f32[8,256]{1,0:T(8,128)}, f32[3,256]{1,0:T(4,128)}, f32[1,8]{1,0:T(1,128)}) custom-call(f32[2,12,512]{2,1,0:T(8,128)} %all-gather.3.shares_ref), custom_call_target="tpu_custom_call" | custom-call | tf_op jit(solution)/shard_map/finish/pallas_call | solution.py:327
  (8 shorter events, 0.1 us)
Async XLA Ops:
  25.2 17.2 %all-to-all-start.1 = ((f32[16,1,640]{2,1,0:T(1,128)}), f32[16,1,640]{2,1,0:T(1,128)S(1)}, u32[]{:S(2)}, u32[]{:S(2)}) async-start(f32[16,1,640]{2,1,0:T(1,128)} %broadcast_in_dim.6), calls=%async_computation.1 | async-start | bytes 81920 | tf_op jit(solution)/shard_map/all_to_all | solution.py:356
